TPU v7x, 512 devices: a whole 4x8x8 slice. The times are simulated.
512 devices in a mesh: expert: 8 (over z_hi, core), dp: 64 (over z_lo, y, x).
Axes of the slice: x: 4, y: 8, z: 8 (z_hi: 4, z_lo: 2; z = z_hi * 2 + z_lo), core: 2. Of those that a mesh axis runs over, the one named last changes fastest.
Arguments:
- hidden: bfloat16 [8, 1024, 8192], P('expert', None, 'dp'), may hold values from -0.1875 to 0.1875
- out_grad: bfloat16 [8, 1024, 6144], P('expert', 'dp'), may hold values from -16 to 16
- gate_weight: float32 [8, 1024], P('expert'), may hold values from 0.1 to 1
- counts: int32 [8], P('expert'), may hold values from 512 to 1024
- carried_error: bfloat16 [8, 8192, 6144], P('expert', 'dp'), may hold values from -40 to 40
- old_query: float32 [6144, 32], P('dp'), may hold values from -6 to 6
Outputs:
- new_error: bfloat16 [8, 8192, 6144], P('expert', 'dp')
- new_query: float32 [6144, 32], P('dp')
Inputs may be any that keep to these rules, and one draw needn't show every extreme that they name: In every draw at least one replica has all its slots live.
All inputs are finite; a program needn't handle non-finite values.
Results may differ from a plain program's by a relative error of at most 0.0034.
Values may be sent and summed in bfloat16 or wider, within the bound.
No kernel may reach another device: no remote copies, remote signals or barrier semaphores. Data moves between devices by JAX's collectives and lax.ppermute only.
A program may use at most 64 MiB of HBM per device.

v0:
```python
import jax
import jax.numpy as jnp
from jax import lax
from jax.sharding import PartitionSpec as P

exact_mode = lax.Precision.HIGHEST


def right_solve(chol_lower, values):
    return lax.linalg.triangular_solve(
        chol_lower, values, left_side=False, lower=True, transpose_a=True
    )


def contract_rows(left_side, right_side, mode):
    return lax.dot_general(
        left_side,
        right_side,
        (((0,), (0,)), ((), ())),
        precision=mode,
        preferred_element_type=jnp.float32,
    )


def body(hidden, out_grad, gate_weight, counts, carried_error, old_query):
    hidden_local = hidden[0]
    grad_rows = out_grad[0]
    gate_local = gate_weight[0]
    error_local = carried_error[0]
    slot_total = hidden_local.shape[0]
    query_rows = old_query.shape[0]
    replicas = lax.axis_size("expert")
    live_slots = lax.iota(jnp.int32, slot_total) < counts[0]
    slot_scale = jnp.where(live_slots, gate_local, jnp.zeros_like(gate_local))
    weighted = (hidden_local.astype(jnp.float32) * slot_scale[:, None]).astype(jnp.bfloat16)
    query_low = old_query.astype(jnp.bfloat16)
    full_query = lax.all_gather(query_low, "dp", axis=0, tiled=True)
    error_wide = error_local.astype(jnp.float32)
    merged = (
        contract_rows(weighted, lax.all_gather(grad_rows, "dp", axis=0, tiled=True), None)
        + error_wide
    )
    left_part = jnp.dot(merged, full_query.astype(jnp.float32), precision=exact_mode)
    left_sum = lax.psum(left_part, "expert") / replicas
    gram_matrix = lax.psum(jnp.dot(left_sum.T, left_sum, precision=exact_mode), "dp")
    chol_lower = jnp.linalg.cholesky(gram_matrix)
    left_basis = right_solve(chol_lower, left_sum)
    query_part = contract_rows(merged, left_basis, exact_mode)
    full_sum = lax.psum(query_part, ("expert", "dp")) / replicas
    new_rows = lax.dynamic_slice_in_dim(full_sum, lax.axis_index("dp") * query_rows, query_rows, 0)
    correction = jnp.dot(left_basis, full_sum.T, precision=exact_mode)
    new_error = (merged - correction).astype(jnp.bfloat16)
    return (new_error[None], new_rows)


def solution(mesh):
    in_specs = (
        P("expert", None, "dp"),
        P("expert", "dp", None),
        P("expert", None),
        P("expert"),
        P("expert", "dp", None),
        P("dp", None),
    )
    out_specs = (P("expert", "dp", None), P("dp", None))
    return jax.shard_map(body, mesh=mesh, in_specs=in_specs, out_specs=out_specs, check_vma=False)
```

profile of v0, /device:TPU:1, one launch (start us, length us, event | category | flops | bytes accessed | tf_op | source)
XLA Modules:
  0.0 973.7 jit_solution(6690158624699583265)
XLA Ops:
  7.2 0.0 all-gather.4.cloned.1.call-start
  7.2 0.7 all-gather.4.cloned.1.call-update
  7.9 0.0 all-reduce.2.cloned.1.call-start
  8.6 0.7 convert_bitcast_fusion
  9.3 138.3 %all-gather.1 = bf16[64,96,32]{1,2,0:T(8,128)(2,1)S(1)} all-gather(bf16[1,96,32]{1,2,0:T(8,128)(2,1)S(1)} %convert_bitcast_fusion), channel_id=1, replica_groups=mesh['expert'=8,'dp'=64] {'dp'}, dimensions={0}, use_global_device_ids=true | all-gather | bytes 399360 | tf_op jit(solution)/shard_map/all_gather | solution.py:37
  147.6 0.2 copy.13
  147.8 0.7 reshape.30
  148.5 0.7 fusion.20
  149.2 152.9 %all-gather.4.cloned.1.call-done = bf16[1,1024,6144]{2,1,0:T(8,128)(2,1)} async-done(((bf16[1,16,6144]{2,1,0:T(8,128)(2,1)}), bf16[1,1024,6144]{2,1,0:T(8,128)(2,1)}) %all-gather.4.cloned.1.call-update) | async-done | bytes 12582928 | tf_op jit(solution)/shard_map/all_gather | solution.py:40
  302.2 7.0 fusion.2
  309.2 1.8 fusion.23
  311.0 64.0 %psum.21 = f32[128,32]{0,1:T(8,128)S(1)} all-reduce(f32[128,32]{0,1:T(8,128)S(1)} %fusion.23), channel_id=1, replica_groups=mesh['expert'=8,'dp'=64] {'expert'}, use_global_device_ids=true, to_apply=%region_0.1 | all-reduce | flops 4096 | bytes 32768 | tf_op jit(solution)/shard_map/psum | solution.py:44
  375.0 0.1 fusion.16
  375.2 252.6 %psum.22 = f32[32,32]{0,1:T(8,128)S(1)} all-reduce(f32[32,32]{0,1:T(8,128)S(1)} %fusion.16), channel_id=1, replica_groups=mesh['expert'=8,'dp'=64] {'dp'}, use_global_device_ids=true, to_apply=%region_1.2 | all-reduce | flops 1024 | bytes 8192 | tf_op jit(solution)/shard_map/psum | solution.py:45
  627.8 0.1 copy.15
  627.9 2.9 cholesky.16
  630.8 0.6 compare_reduce_fusion
  631.5 0.7 fusion.11
  632.1 2.4 custom-call.6
  634.6 0.2 fusion.12
  634.8 2.7 fusion.24
  637.6 0.0 all-reduce.2.cloned.1.call-update
  637.6 322.5 %all-reduce.2.cloned.1.call-done = f32[6144,32]{0,1:T(8,128)} async-done(((f32[6144,32]{0,1:T(8,128)}), f32[6144,32]{0,1:T(8,128)}) %all-reduce.2.cloned.1.call-update) | async-done | bytes 786448 | tf_op jit(solution)/shard_map/psum | solution.py:49
  960.0 1.2 broadcast_multiply_fusion
  961.2 0.7 constant_dynamic-slice_fusion
  961.9 5.0 fusion.6
  (2 shorter events, 0.0 us)
Async XLA Ops:
  7.2 295.0 %all-gather.4.cloned.1.call-start = ((), (), s32[]{:S(2)}) async-start(), calls=%async_computation.1 | async-start | bytes 12779520 | tf_op jit(solution)/shard_map/all_gather | solution.py:40
  7.9 952.1 %all-reduce.2.cloned.1.call-start = ((), (), s32[]{:S(2)}) async-start(), calls=%async_computation | async-start | bytes 1572864 | tf_op jit(solution)/shard_map/psum | solution.py:49
Sparse Core Ops, SparseCore 0:
  10.1 292.0 all-gather.3
  637.7 322.2 all-reduce.1
where the time goes:
time: 974 us
  waiting for transfers between devices  476 us (49%)
  blocking collectives  455 us (47%)
  matrix products  17 us (2%)
  between operations  14.7 us (2%)
    psum x1, waiting for transfers between devices, body(): full_sum = lax.psum(query_part, ('expert', 'dp')) / replicas  322 us
    psum x1, blocking collectives, body(): lax.psum(jnp.dot(left_sum.T, left_sum, precision=exact_mode), 'dp')  253 us
    all_gather x1, waiting for transfers between devices, body(): lax.all_gather(grad_rows, 'dp', axis=0, tiled=True)  153 us
    all_gather x1, blocking collectives, body(): full_query = lax.all_gather(query_low, 'dp', axis=0, tiled=True)  138 us
    psum x1, blocking collectives, body(): left_sum = lax.psum(left_part, 'expert') / replicas  64 us
  transfers between devices with their start and end apart: 2, of which 2 were waited for; matrix products, arithmetic and copies ran while one was open for 0% of the time, Pallas kernels for 0%

commit v1 on v0

v1 whole, which is shorter than its diff:
```python
import jax
import jax.numpy as jnp
from jax import lax
from jax.sharding import Mesh, PartitionSpec as P

EXPERT = ("zh", "core")
DP = ("zl", "y", "x")
PLANE = ("y", "x")
exact_mode = lax.Precision.HIGHEST
f32 = jnp.float32
bf16 = jnp.bfloat16


def exchange(blocks, axes):
    return lax.all_to_all(blocks, axes, split_axis=0, concat_axis=0, tiled=True)


def spread(block, axes, count):
    return exchange(jnp.broadcast_to(block[None], (count,) + block.shape), axes)


def halves(values):
    high = lax.reduce_precision(values, 8, 7)
    return high.astype(bf16), (values - high).astype(bf16)


def product(left_side, right_side, left_dim, right_dim):
    return lax.dot_general(
        left_side,
        right_side,
        (((left_dim,), (right_dim,)), ((), ())),
        preferred_element_type=f32,
    )


def body(hidden, out_grad, gate_weight, counts, carried_error, old_query):
    hidden_local = hidden[0]
    grad_rows = out_grad[0]
    error_local = carried_error[0]
    slots, units = hidden_local.shape
    own_slots, width = grad_rows.shape
    own_rows, rank = old_query.shape
    replicas = lax.axis_size(EXPERT)
    members = lax.axis_size(DP)
    plane = lax.axis_size(PLANE)
    pair = lax.axis_size("zl")

    query_low = old_query.astype(bf16)
    query_blocks = spread(query_low.T, DP, members)
    full_query = query_blocks.transpose(1, 0, 2).reshape(rank, width)

    pair_rows = lax.all_gather(grad_rows, "zl", axis=0, tiled=True)
    full_grad = lax.all_gather(pair_rows, PLANE, axis=0, tiled=True)

    live_slots = lax.iota(jnp.int32, slots) < counts[0]
    slot_scale = jnp.where(live_slots, gate_weight[0], jnp.zeros_like(gate_weight[0]))
    weighted = (hidden_local.astype(f32) * slot_scale[:, None]).astype(bf16)

    slot_query = product(grad_rows, full_query, 1, 1)
    all_slots = spread(slot_query, DP, members).reshape(slots, rank)
    slot_pair = jnp.concatenate(halves(all_slots), axis=1)
    left_pair = product(weighted, slot_pair, 0, 0)
    left_part = left_pair[:, :rank] + left_pair[:, rank:] + product(error_local, full_query, 1, 1)
    left_sum = jnp.sum(spread(left_part, EXPERT, replicas), axis=0) / replicas

    sum_pair = jnp.concatenate(halves(left_sum), axis=1)
    slot_parts = product(weighted, sum_pair, 1, 0)
    slot_parts = slot_parts[:, :rank] + slot_parts[:, rank:]
    gram_part = lax.dot_general(
        left_sum, left_sum, (((0,), (0,)), ((), ())), precision=exact_mode, preferred_element_type=f32
    )
    outgoing = jnp.concatenate(
        [
            slot_parts.reshape(members, own_slots, rank),
            jnp.broadcast_to(gram_part[None], (members, rank, rank)),
        ],
        axis=1,
    )
    summed = jnp.sum(exchange(outgoing, DP), axis=0)
    own_vectors = summed[:own_slots]
    gram_matrix = summed[own_slots:]

    vector_pair = jnp.concatenate(halves(own_vectors), axis=1)
    query_pair = product(vector_pair, grad_rows, 0, 0) + product(sum_pair, error_local, 0, 0)
    query_part = query_pair[:rank] + query_pair[rank:]
    query_part = query_part.reshape(rank, members, own_rows).transpose(1, 0, 2)
    own_part = jnp.sum(exchange(query_part, DP), axis=0)
    own_sum = jnp.sum(spread(own_part, EXPERT, replicas), axis=0) / replicas

    chol_lower = jnp.linalg.cholesky(gram_matrix)
    inverse = lax.linalg.triangular_solve(
        chol_lower, jnp.eye(rank, dtype=f32), left_side=True, lower=True
    )
    left_basis = lax.dot_general(
        left_sum, inverse, (((1,), (1,)), ((), ())), precision=exact_mode, preferred_element_type=f32
    )
    new_cols = jnp.dot(inverse, own_sum, precision=exact_mode, preferred_element_type=f32)
    new_rows = new_cols.T
    all_cols = spread(new_cols, DP, members).transpose(1, 0, 2).reshape(rank, width)

    basis_high, basis_low = halves(left_basis)
    cols_high, cols_low = halves(all_cols)
    correction = product(
        jnp.concatenate([basis_high, basis_low, basis_high], axis=1),
        jnp.concatenate([cols_high, cols_high, cols_low], axis=0),
        1,
        0,
    )
    ordered = weighted.reshape(pair, plane, own_slots, units).transpose(1, 0, 2, 3).reshape(slots, units)
    local_grad = product(ordered, full_grad, 0, 0)
    new_error = (local_grad + error_local.astype(f32) - correction).astype(bf16)
    return (new_error[None], new_rows)


def solution(mesh):
    fine = Mesh(mesh.devices.reshape(4, 2, 2, 8, 4), EXPERT + DP)
    in_specs = (
        P(EXPERT, None, DP),
        P(EXPERT, DP, None),
        P(EXPERT, None),
        P(EXPERT),
        P(EXPERT, DP, None),
        P(DP, None),
    )
    out_specs = (P(EXPERT, DP, None), P(DP, None))
    return jax.shard_map(body, mesh=fine, in_specs=in_specs, out_specs=out_specs, check_vma=False)
```

time: 974 us -> 246 us (0.25)
  blocking collectives: 455 us -> 59.5 us
  waiting for transfers between devices: 476 us -> 89.3 us
  starting transfers between devices: 0.08 us -> 32.6 us
  local copies, waits for them, and re-layouts: 1.69 us -> 18.5 us
    psum x1 -> x0, waiting for transfers between devices: 322 us -> none  [body(): full_sum = lax.psum(query_part, ('expert', 'dp')) / replicas]
    psum x2 -> x0, blocking collectives: 317 us -> none  [the longest x1 253 us: body(): lax.psum(jnp.dot(left_sum.T, left_sum, precision=exact_mode), 'dp')]
    all_gather x1, waiting for transfers between devices: 153 us -> 0.02 us  [body(): full_grad = lax.all_gather(pair_rows, PLANE, axis=0, tiled=True)]
    all_gather x1, blocking collectives: 138 us -> 8.56 us  [body(): pair_rows = lax.all_gather(grad_rows, 'zl', axis=0, tiled=True)]
    all_to_all x0 -> x5, waiting for transfers between devices: none -> 89.3 us  [exchange(): return lax.all_to_all(blocks, axes, split_axis=0, concat_axis=0, tiled=True)]
    all_to_all x0 -> x2, blocking collectives: none -> 50.9 us  [exchange(): return lax.all_to_all(blocks, axes, split_axis=0, concat_axis=0, tiled=True)]
    all_to_all x0 -> x5, starting transfers between devices: none -> 32.5 us  [exchange(): return lax.all_to_all(blocks, axes, split_axis=0, concat_axis=0, tiled=True)]
  transfers between devices with their start and end apart: 2 -> 6, of which waited for: 2 -> 5; matrix products, arithmetic and copies ran while one was open for 0% -> 15% of each run, Pallas kernels for 0% -> 0%
where the time goes in v1:
time: 246 us; the launch traced here: 242 us
  waiting for transfers between devices  89.3 us (36%)
  blocking collectives  59.5 us (24%)
  starting transfers between devices  32.6 us (13%)
  local copies, waits for them, and re-layouts  18.5 us (8%)
  other arithmetic  15.8 us (6%)
  between operations  15 us (6%)
  matrix products  11.6 us (5%)
    all_to_all x5, waiting for transfers between devices, exchange(): return lax.all_to_all(blocks, axes, split_axis=0, concat_axis=0, tiled=True)  89.3 us
    all_to_all x2, blocking collectives, exchange(): return lax.all_to_all(blocks, axes, split_axis=0, concat_axis=0, tiled=True)  50.9 us
    all_to_all x5, starting transfers between devices, exchange(): return lax.all_to_all(blocks, axes, split_axis=0, concat_axis=0, tiled=True)  32.5 us
    dot_general x8, matrix products, product(): lax.dot_general(left_side, right_side, (((left_dim,), (right_dim,)), ((),...  11 us
    unnamed x21, local copies, waits for them, and re-layouts  8.87 us
    all_gather x1, blocking collectives, body(): pair_rows = lax.all_gather(grad_rows, 'zl', axis=0, tiled=True)  8.56 us
  transfers between devices with their start and end apart: 6, of which 5 were waited for; matrix products, arithmetic and copies ran while one was open for 15% of the time, Pallas kernels for 0%

profile of v1, /device:TPU:1, one launch (start us, length us, event | category | flops | bytes accessed | tf_op | source)
XLA Modules:
  0.0 242.2 jit_solution(16773978355940687475)
XLA Ops:
  7.2 8.6 %all-gather = bf16[1,32,6144]{2,1,0:T(8,128)(2,1)} all-gather(bf16[1,16,6144]{2,1,0:T(8,128)(2,1)} %param.7), channel_id=2, replica_groups=mesh['zh'=4,'core'=2,'zl'=2,'y'=8,'x'=4] {'zl'}, dimensions={1}, use_global_device_ids=true | all-gather | bytes 589824 | tf_op jit(solution)/shard_map/all_gather | solution.py:52
  15.8 0.7 convert_bitcast_fusion
  16.6 26.9 %all_to_all.35 = bf16[64,32,96]{2,1,0:T(8,128)(2,1)S(1)} all-to-all(bf16[64,32,96]{2,1,0:T(8,128)(2,1)S(1)} %broadcast_in_dim.21), channel_id=1, replica_groups=mesh['zh'=4,'core'=2,'zl'=2,'y'=8,'x'=4] {'zl','y','x'}, dimensions={0} | all-to-all | bytes 786432 | tf_op jit(solution)/shard_map/all_to_all | solution.py:15
  43.5 0.2 copy.50
  43.8 0.7 reshape.60
  44.5 0.2 fusion.27
  44.8 0.9 reshape.78
  45.7 7.4 %all-to-all-start.1 = ((f32[64,1,512]{2,1,0:T(1,128)}), f32[64,1,512]{2,1,0:T(1,128)S(1)}, u32[]{:S(2)}, u32[]{:S(2)}) async-start(f32[64,1,512]{2,1,0:T(1,128)} %reshape.78), calls=%async_computation.1 | async-start | bytes 262144 | tf_op jit(solution)/shard_map/all_to_all | solution.py:15
  53.7 10.1 %all-to-all-done.1 = f32[64,1,512]{2,1,0:T(1,128)S(1)} async-done(((f32[64,1,512]{2,1,0:T(1,128)}), f32[64,1,512]{2,1,0:T(1,128)S(1)}, u32[]{:S(2)}, u32[]{:S(2)}) %all-to-all-start.1) | async-done | bytes 131104 | tf_op jit(solution)/shard_map/all_to_all | solution.py:15
  63.9 0.5 broadcast.74
  64.4 0.9 reduce.10
  65.3 0.2 reshape.79
  65.5 0.1 reduce-precision_convert_fusion.1
  65.6 0.5 fusion.23
  66.1 0.6 fusion.16
  66.8 24.0 %all_to_all.36 = f32[8,128,32]{1,2,0:T(8,128)S(1)} all-to-all(f32[8,128,32]{1,2,0:T(8,128)S(1)} %broadcast_in_dim.24), channel_id=1, replica_groups=mesh['zh'=4,'core'=2,'zl'=2,'y'=8,'x'=4] {'zh','core'}, dimensions={0} | all-to-all | bytes 262144 | tf_op jit(solution)/shard_map/all_to_all | solution.py:15
  90.8 0.3 fusion.30
  91.2 0.2 copy.51
  91.4 0.4 copy.53
  91.7 0.1 fusion.50
  91.9 0.1 broadcast_in_dim.25
  92.0 1.3 fusion.67
  93.3 3.0 %reshape.80 = f32[64,1,1536]{2,1,0:T(1,128)} reshape(f32[64,32,48]{2,1,0:T(8,128)} %fusion.67) | data formatting | bytes 786432
  96.3 5.4 %all-to-all-start.3 = ((f32[64,1,1536]{2,1,0:T(1,128)}), f32[64,1,1536]{2,1,0:T(1,128)}, u32[]{:S(2)}, u32[]{:S(2)}) async-start(f32[64,1,1536]{2,1,0:T(1,128)} %reshape.80), calls=%async_computation.3 | async-start | bytes 786432 | tf_op jit(solution)/shard_map/all_to_all | solution.py:15
  101.8 0.4 fusion.7
  102.1 16.3 %all-to-all-done.3 = f32[64,1,1536]{2,1,0:T(1,128)} async-done(((f32[64,1,1536]{2,1,0:T(1,128)}), f32[64,1,1536]{2,1,0:T(1,128)}, u32[]{:S(2)}, u32[]{:S(2)}) %all-to-all-start.3) | async-done | bytes 393248 | tf_op jit(solution)/shard_map/all_to_all | solution.py:15
  118.4 3.4 %reduce.11 = f32[64,1536]{1,0:T(8,128)} reduce(f32[64,1,1536]{2,1,0:T(1,128)} %all-to-all-done.3, f32[]{:T(128)} %broadcast.74), dimensions={1}, to_apply=%all_to_all.24.reduce_sub_computation | reduce | bytes 786436 | tf_op jit(solution)/shard_map/all_to_all | solution.py:15
  121.8 2.4 %reshape.81 = f32[64,32,48]{2,1,0:T(8,128)} reshape(f32[64,1536]{1,0:T(8,128)} %reduce.11) | data formatting | bytes 786432
  124.2 1.3 bitcast_reduce_fusion
  125.6 0.1 copy.56
  125.6 0.1 copy.55
  125.7 0.5 convolution_add_fusion
  126.2 0.1 slice_add_fusion
  126.3 0.4 reshape.63
  126.7 1.6 copy.61
  128.3 6.9 %all-to-all-start.4 = ((f32[64,32,96]{2,1,0:T(8,128)}), f32[64,32,96]{2,1,0:T(8,128)S(1)}, u32[]{:S(2)}, u32[]{:S(2)}) async-start(f32[64,32,96]{2,1,0:T(8,128)} %bitcast.66), calls=%async_computation.4 | async-start | bytes 2097152 | tf_op jit(solution)/shard_map/all_to_all | solution.py:15
  135.3 0.1 copy.54
  135.3 0.1 fusion.45
  135.4 2.9 %cholesky.17 = f32[32,32]{1,0:T(8,128)S(1)} custom-call(f32[32,32]{1,0:T(8,128)S(1)} %fusion.45), custom_call_target="Cholesky" | custom-call | tf_op jit(solution)/shard_map/jit(cholesky)/cholesky | solution.py:90
  138.4 0.6 compare_reduce_fusion
  139.0 0.7 fusion.39
  139.7 2.4 %custom-call.6 = f32[1,32,32]{1,2,0:T(8,128)S(1)} custom-call(f32[1,32,32]{2,1,0:T(8,128)S(1)} %fusion.39), custom_call_target="InvertDiagBlocksLowerTriangular" | custom-call | tf_op jit(solution)/shard_map/triangular_solve | solution.py:91
  142.1 31.6 %all-to-all-done.4 = f32[64,32,96]{2,1,0:T(8,128)S(1)} async-done(((f32[64,32,96]{2,1,0:T(8,128)}), f32[64,32,96]{2,1,0:T(8,128)S(1)}, u32[]{:S(2)}, u32[]{:S(2)}) %all-to-all-start.4) | async-done | bytes 786464 | tf_op jit(solution)/shard_map/all_to_all | solution.py:15
  173.7 0.1 reduce_sum.38
  173.8 0.7 broadcast_in_dim.26
  174.5 7.2 %all-to-all-start.5 = ((f32[8,32,96]{2,1,0:T(8,128)}), f32[8,32,96]{2,1,0:T(8,128)S(1)}, u32[]{:S(2)}, u32[]{:S(2)}) async-start(f32[8,32,96]{2,1,0:T(8,128)} %broadcast_in_dim.26), calls=%async_computation.5 | async-start | bytes 262144 | tf_op jit(solution)/shard_map/all_to_all | solution.py:15
  181.7 0.2 fusion.43
  181.9 7.8 %all-to-all-done.5 = f32[8,32,96]{2,1,0:T(8,128)S(1)} async-done(((f32[8,32,96]{2,1,0:T(8,128)}), f32[8,32,96]{2,1,0:T(8,128)S(1)}, u32[]{:S(2)}, u32[]{:S(2)}) %all-to-all-start.5) | async-done | bytes 98336 | tf_op jit(solution)/shard_map/all_to_all | solution.py:15
  189.7 0.1 fusion.46
  189.9 1.1 broadcast_in_dim.27
  191.0 5.7 %all-to-all-start.6 = ((f32[64,32,96]{2,1,0:T(8,128)}), f32[64,32,96]{2,1,0:T(8,128)S(1)}, u32[]{:S(2)}, u32[]{:S(2)}) async-start(f32[64,32,96]{2,1,0:T(8,128)} %broadcast_in_dim.27), calls=%async_computation.6 | async-start | bytes 2097152 | tf_op jit(solution)/shard_map/all_to_all | solution.py:15
  196.7 0.6 broadcast.73
  197.2 0.7 reduce.9
  198.0 0.2 fusion.22
  198.2 0.7 copy.49
  199.0 0.1 fusion.41
  199.1 23.4 %all-to-all-done.6 = f32[64,32,96]{2,1,0:T(8,128)S(1)} async-done(((f32[64,32,96]{2,1,0:T(8,128)}), f32[64,32,96]{2,1,0:T(8,128)S(1)}, u32[]{:S(2)}, u32[]{:S(2)}) %all-to-all-start.6) | async-done | bytes 786464 | tf_op jit(solution)/shard_map/all_to_all | solution.py:15
  222.5 1.0 copy-done.1
  223.5 1.8 copy.58
  225.3 0.6 reshape.64
  226.0 0.1 reduce-precision_convert_fusion
  226.1 0.8 copy-done.5
  226.9 6.7 %fusion.2 = f32[128,6144]{1,0:T(8,128)S(1)} fusion(bf16[1024,128]{1,0:T(8,128)(2,1)S(1)} %bitcast.70, bf16[1,1024,6144]{2,1,0:T(8,128)(2,1)} %all-gather.4.cloned.1.call-done, bf16[1,128,6144]{2,1,0:T(8,128)(2,1)S(1)} %copy-done), kind=kOutput, calls=%fused_computation.3 | convolution fusion | flops 1612185600 | bytes 17563648 | tf_op jit(solution)/shard_map/dot_general | solution.py:28
  233.6 1.8 fusion.6
  (30 shorter events, 0.5 us)
Async XLA Ops:
  7.2 218.9 %all-gather.4.cloned.1.call-start = ((), (), s32[]{:S(2)}) async-start(), calls=%async_computation.7 | async-start | bytes 12976128 | tf_op jit(solution)/shard_map/all_gather | solution.py:53
  16.6 27.9 %copy-start.4 = (bf16[1,16,6144]{2,1,0:T(8,128)(2,1)S(1)}, bf16[1,16,6144]{2,1,0:T(8,128)(2,1)}, u32[]{:S(2)}) copy-start(bf16[1,16,6144]{2,1,0:T(8,128)(2,1)} %param.7) | copy-start | bytes 589828
  43.7 9.9 %copy-start.7 = (f32[1,1024]{1,0:T(1,128)S(1)}, f32[1,1024]{1,0:T(1,128)}, u32[]{:S(2)}) copy-start(f32[1,1024]{1,0:T(1,128)} %param.8) | copy-start | bytes 12292
  44.8 20.8 %copy-start.2 = (bf16[1,1024,128]{2,1,0:T(8,128)(2,1)S(1)}, bf16[1,1024,128]{2,1,0:T(8,128)(2,1)}, u32[]{:S(2)}) copy-start(bf16[1,1024,128]{2,1,0:T(8,128)(2,1)} %param.6) | copy-start | bytes 786436
  45.7 20.5 %copy-start = (bf16[1,128,6144]{2,1,0:T(8,128)(2,1)S(1)}, bf16[1,128,6144]{2,1,0:T(8,128)(2,1)}, u32[]{:S(2)}) copy-start(bf16[1,128,6144]{2,1,0:T(8,128)(2,1)} %param.10) | copy-start | bytes 4718596
  45.7 18.2 %all-to-all-start.1 = ((f32[64,1,512]{2,1,0:T(1,128)}), f32[64,1,512]{2,1,0:T(1,128)S(1)}, u32[]{:S(2)}, u32[]{:S(2)}) async-start(f32[64,1,512]{2,1,0:T(1,128)} %reshape.78), calls=%async_computation.1 | async-start | bytes 262144 | tf_op jit(solution)/shard_map/all_to_all | solution.py:15
  96.3 22.1 %all-to-all-start.3 = ((f32[64,1,1536]{2,1,0:T(1,128)}), f32[64,1,1536]{2,1,0:T(1,128)}, u32[]{:S(2)}, u32[]{:S(2)}) async-start(f32[64,1,1536]{2,1,0:T(1,128)} %reshape.80), calls=%async_computation.3 | async-start | bytes 786432 | tf_op jit(solution)/shard_map/all_to_all | solution.py:15
  128.3 45.4 %all-to-all-start.4 = ((f32[64,32,96]{2,1,0:T(8,128)}), f32[64,32,96]{2,1,0:T(8,128)S(1)}, u32[]{:S(2)}, u32[]{:S(2)}) async-start(f32[64,32,96]{2,1,0:T(8,128)} %bitcast.66), calls=%async_computation.4 | async-start | bytes 2097152 | tf_op jit(solution)/shard_map/all_to_all | solution.py:15
  174.5 15.2 %all-to-all-start.5 = ((f32[8,32,96]{2,1,0:T(8,128)}), f32[8,32,96]{2,1,0:T(8,128)S(1)}, u32[]{:S(2)}, u32[]{:S(2)}) async-start(f32[8,32,96]{2,1,0:T(8,128)} %broadcast_in_dim.26), calls=%async_computation.5 | async-start | bytes 262144 | tf_op jit(solution)/shard_map/all_to_all | solution.py:15
  189.9 1.1 copy-start.6
  189.9 8.1 %copy-start.3 = (bf16[1,1024,128]{2,1,0:T(8,128)(2,1)S(1)}, bf16[1,1024,128]{2,1,0:T(8,128)(2,1)}, u32[]{:S(2)}) copy-start(bf16[1,1024,128]{2,1,0:T(8,128)(2,1)} %param.6) | copy-start | bytes 786436
  191.0 31.5 %all-to-all-start.6 = ((f32[64,32,96]{2,1,0:T(8,128)}), f32[64,32,96]{2,1,0:T(8,128)S(1)}, u32[]{:S(2)}, u32[]{:S(2)}) async-start(f32[64,32,96]{2,1,0:T(8,128)} %broadcast_in_dim.27), calls=%async_computation.6 | async-start | bytes 2097152 | tf_op jit(solution)/shard_map/all_to_all | solution.py:15
  222.5 1.0 copy-start.1
  225.9 1.0 copy-start.5
Sparse Core Ops, SparseCore 0:
  15.9 162.8 all-gather.3

commit v2 on v1

--- a/solution.py
+++ b/solution.py
@@ -43,43 +43,45 @@
     replicas = lax.axis_size(EXPERT)
     members = lax.axis_size(DP)
     plane = lax.axis_size(PLANE)
-    pair = lax.axis_size("zl")
 
     query_low = old_query.astype(bf16)
     query_blocks = spread(query_low.T, DP, members)
+    partner_rows = lax.ppermute(grad_rows, "zl", [(0, 1), (1, 0)])
+    pair_rows = jnp.concatenate([grad_rows, partner_rows], axis=0)
+    query_blocks, pair_rows = lax.optimization_barrier((query_blocks, pair_rows))
+    full_grad = lax.all_gather(pair_rows, PLANE, axis=0, tiled=True)
     full_query = query_blocks.transpose(1, 0, 2).reshape(rank, width)
-
-    pair_rows = lax.all_gather(grad_rows, "zl", axis=0, tiled=True)
-    full_grad = lax.all_gather(pair_rows, PLANE, axis=0, tiled=True)
 
     live_slots = lax.iota(jnp.int32, slots) < counts[0]
     slot_scale = jnp.where(live_slots, gate_weight[0], jnp.zeros_like(gate_weight[0]))
     weighted = (hidden_local.astype(f32) * slot_scale[:, None]).astype(bf16)
 
     slot_query = product(grad_rows, full_query, 1, 1)
-    all_slots = spread(slot_query, DP, members).reshape(slots, rank)
-    slot_pair = jnp.concatenate(halves(all_slots), axis=1)
+    slot_pair = spread(jnp.concatenate(halves(slot_query), axis=1), DP, members).reshape(slots, 2 * rank)
     left_pair = product(weighted, slot_pair, 0, 0)
     left_part = left_pair[:, :rank] + left_pair[:, rank:] + product(error_local, full_query, 1, 1)
     left_sum = jnp.sum(spread(left_part, EXPERT, replicas), axis=0) / replicas
 
-    sum_pair = jnp.concatenate(halves(left_sum), axis=1)
-    slot_parts = product(weighted, sum_pair, 1, 0)
-    slot_parts = slot_parts[:, :rank] + slot_parts[:, rank:]
+    sum_high, sum_low = halves(left_sum)
+    slot_parts = product(
+        jnp.concatenate([weighted, weighted], axis=1), jnp.concatenate([sum_high, sum_low], axis=0), 1, 0
+    )
     gram_part = lax.dot_general(
         left_sum, left_sum, (((0,), (0,)), ((), ())), precision=exact_mode, preferred_element_type=f32
     )
+    gram_wide = jnp.concatenate([gram_part[:own_slots], gram_part[own_slots:]], axis=1)
     outgoing = jnp.concatenate(
         [
             slot_parts.reshape(members, own_slots, rank),
-            jnp.broadcast_to(gram_part[None], (members, rank, rank)),
+            jnp.broadcast_to(gram_wide[None], (members,) + gram_wide.shape),
         ],
-        axis=1,
+        axis=2,
     )
     summed = jnp.sum(exchange(outgoing, DP), axis=0)
-    own_vectors = summed[:own_slots]
-    gram_matrix = summed[own_slots:]
+    own_vectors = summed[:, :rank]
+    gram_matrix = jnp.concatenate([summed[:, rank : 2 * rank], summed[:, 2 * rank :]], axis=0)
 
+    sum_pair = jnp.concatenate([sum_high, sum_low], axis=1)
     vector_pair = jnp.concatenate(halves(own_vectors), axis=1)
     query_pair = product(vector_pair, grad_rows, 0, 0) + product(sum_pair, error_local, 0, 0)
     query_part = query_pair[:rank] + query_pair[rank:]
@@ -96,19 +98,23 @@
     )
     new_cols = jnp.dot(inverse, own_sum, precision=exact_mode, preferred_element_type=f32)
     new_rows = new_cols.T
-    all_cols = spread(new_cols, DP, members).transpose(1, 0, 2).reshape(rank, width)
+    col_blocks = spread(jnp.concatenate(halves(new_cols), axis=0), DP, members)
 
+    own_first = lax.axis_index("zl") == 0
+    parts = weighted.reshape(2, plane, own_slots, units)
+    ordered = jnp.where(
+        own_first,
+        jnp.stack([parts[0], parts[1]], axis=1),
+        jnp.stack([parts[1], parts[0]], axis=1),
+    ).reshape(slots, units)
+    merged = product(ordered, full_grad, 0, 0) + error_local.astype(f32)
+    merged, col_blocks = lax.optimization_barrier((merged, col_blocks))
+    col_pair = col_blocks.transpose(1, 0, 2).reshape(2 * rank, width)
     basis_high, basis_low = halves(left_basis)
-    cols_high, cols_low = halves(all_cols)
     correction = product(
-        jnp.concatenate([basis_high, basis_low, basis_high], axis=1),
-        jnp.concatenate([cols_high, cols_high, cols_low], axis=0),
-        1,
-        0,
-    )
-    ordered = weighted.reshape(pair, plane, own_slots, units).transpose(1, 0, 2, 3).reshape(slots, units)
-    local_grad = product(ordered, full_grad, 0, 0)
-    new_error = (local_grad + error_local.astype(f32) - correction).astype(bf16)
+        jnp.concatenate([basis_high, basis_high], axis=1), col_pair, 1, 0
+    ) + product(basis_low, col_pair[:rank], 1, 0)
+    new_error = (merged - correction).astype(bf16)
     return (new_error[None], new_rows)
 
 

time: 246 us -> 226 us (0.919)
  blocking collectives: 59.5 us -> 0 us
  starting transfers between devices: 32.6 us -> 60.7 us
  waiting for transfers between devices: 89.3 us -> 110 us
  local copies, waits for them, and re-layouts: 18.5 us -> 12.1 us
  other arithmetic: 15.8 us -> 11.2 us
    all_to_all x2 -> x0, blocking collectives: 50.9 us -> none  [exchange(): return lax.all_to_all(blocks, axes, split_axis=0, concat_axis=0, tiled=True)]
    all_to_all x5 -> x7, starting transfers between devices: 32.5 us -> 55.7 us  [exchange(): return lax.all_to_all(blocks, axes, split_axis=0, concat_axis=0, tiled=True)]
    all_gather x1, waiting for transfers between devices: 0.02 us -> 21.5 us  [body(): full_grad = lax.all_gather(pair_rows, PLANE, axis=0, tiled=True)]
    all_gather x1 -> x0, blocking collectives: 8.56 us -> none  [body(): pair_rows = lax.all_gather(grad_rows, 'zl', axis=0, tiled=True)]
    unnamed x21 -> x18, local copies, waits for them, and re-layouts: 8.87 us -> 2.53 us
    ppermute x0 -> x1, starting transfers between devices: none -> 4.96 us  [body(): partner_rows = lax.ppermute(grad_rows, 'zl', [(0, 1), (1, 0)])]
    all_to_all x2 -> x0, other arithmetic: 4.3 us -> none  [exchange(): return lax.all_to_all(blocks, axes, split_axis=0, concat_axis=0, tiled=True)]
    dot_general x8 -> x9, matrix products: 11 us -> 12.8 us  [product(): lax.dot_general(left_side, right_side, (((left_dim,), (right_dim,)), ((),...]
  transfers between devices with their start and end apart: 6 -> 9, of which waited for: 5 -> 8; matrix products, arithmetic and copies ran while one was open for 15% -> 14% of each run, Pallas kernels for 0% -> 0%
where the time goes in v2:
time: 226 us; the launch traced here: 223 us
  waiting for transfers between devices  110 us (49%)
  starting transfers between devices  60.7 us (27%)
  between operations  15 us (7%)
  matrix products  14 us (6%)
  local copies, waits for them, and re-layouts  12.1 us (5%)
  other arithmetic  11.2 us (5%)
    all_to_all x7, waiting for transfers between devices, exchange(): return lax.all_to_all(blocks, axes, split_axis=0, concat_axis=0, tiled=True)  88 us
    all_to_all x7, starting transfers between devices, exchange(): return lax.all_to_all(blocks, axes, split_axis=0, concat_axis=0, tiled=True)  55.7 us
    all_gather x1, waiting for transfers between devices, body(): full_grad = lax.all_gather(pair_rows, PLANE, axis=0, tiled=True)  21.5 us
    dot_general x9, matrix products, product(): lax.dot_general(left_side, right_side, (((left_dim,), (right_dim,)), ((),...  12.8 us
    ppermute x1, starting transfers between devices, body(): partner_rows = lax.ppermute(grad_rows, 'zl', [(0, 1), (1, 0)])  4.96 us
  transfers between devices with their start and end apart: 9, of which 8 were waited for; matrix products, arithmetic and copies ran while one was open for 14% of the time, Pallas kernels for 0%

profile of v2, /device:TPU:1, one launch (start us, length us, event | category | flops | bytes accessed | tf_op | source)
XLA Modules:
  0.0 222.6 jit_solution(1848421620417806117)
XLA Ops:
  7.2 5.0 %collective-permute-start = (bf16[16,6144]{1,0:T(8,128)(2,1)}, bf16[16,6144]{1,0:T(8,128)(2,1)S(1)}, u32[]{:S(2)}, u32[]{:S(2)}) collective-permute-start(bf16[16,6144]{1,0:T(8,128)(2,1)} %bitcast.72), channel_id=1, source_target_pairs={{0,32},{32,0},{1,33},{33,1},{2,34},{34,2},{3,35},{35,3},{4,36},{36... | collective-permute-start | bytes 589832 | tf_op jit(solution)/shard_map/ppermute | solution.py:49
  12.1 0.7 convert_bitcast_fusion.1
  12.9 0.9 broadcast_in_dim.18
  13.7 10.3 %all-to-all-start = ((bf16[64,32,96]{2,1,0:T(8,128)(2,1)}), bf16[64,32,96]{2,1,0:T(8,128)(2,1)S(1)}, u32[]{:S(2)}, u32[]{:S(2)}) async-start(bf16[64,32,96]{2,1,0:T(8,128)(2,1)} %broadcast_in_dim.18), calls=%async_computation | async-start | bytes 1048576 | tf_op jit(solution)/shard_map/all_to_all | solution.py:15
  24.0 0.0 all-gather.2.cloned.1.call-start
  24.1 0.8 pad_maximum_fusion.1
  24.9 14.9 %all-to-all-done = bf16[64,32,96]{2,1,0:T(8,128)(2,1)S(1)} async-done(((bf16[64,32,96]{2,1,0:T(8,128)(2,1)}), bf16[64,32,96]{2,1,0:T(8,128)(2,1)S(1)}, u32[]{:S(2)}, u32[]{:S(2)}) %all-to-all-start) | async-done | bytes 393248 | tf_op jit(solution)/shard_map/all_to_all | solution.py:15
  39.8 0.2 copy.22
  40.0 0.7 reshape.64
  40.7 0.2 reduce-precision_convert_fusion.4
  41.0 0.1 pad_maximum_fusion.5
  41.1 0.8 reshape.70
  41.9 6.8 %all-to-all-start.1 = ((bf16[64,2,512]{2,1,0:T(2,128)(2,1)}), bf16[64,2,512]{2,1,0:T(2,128)(2,1)S(1)}, u32[]{:S(2)}, u32[]{:S(2)}) async-start(bf16[64,2,512]{2,1,0:T(2,128)(2,1)} %reshape.70), calls=%async_computation.1 | async-start | bytes 262144 | tf_op jit(solution)/shard_map/all_to_all | solution.py:15
  49.4 9.3 %all-to-all-done.1 = bf16[64,2,512]{2,1,0:T(2,128)(2,1)S(1)} async-done(((bf16[64,2,512]{2,1,0:T(2,128)(2,1)}), bf16[64,2,512]{2,1,0:T(2,128)(2,1)S(1)}, u32[]{:S(2)}, u32[]{:S(2)}) %all-to-all-start.1) | async-done | bytes 131104 | tf_op jit(solution)/shard_map/all_to_all | solution.py:15
  58.7 0.2 reshape.71
  59.0 0.4 fusion.21
  59.4 0.6 fusion.10
  60.0 0.7 broadcast_in_dim.20
  60.7 12.7 %all-to-all-start.2 = ((f32[8,128,32]{1,2,0:T(8,128)}), f32[8,128,32]{1,2,0:T(8,128)S(1)}, u32[]{:S(2)}, u32[]{:S(2)}) async-start(f32[8,128,32]{1,2,0:T(8,128)} %broadcast_in_dim.20), calls=%async_computation.2 | async-start | bytes 262144 | tf_op jit(solution)/shard_map/all_to_all | solution.py:15
  73.4 0.2 fusion.14
  73.6 7.8 %all-to-all-done.2 = f32[8,128,32]{1,2,0:T(8,128)S(1)} async-done(((f32[8,128,32]{1,2,0:T(8,128)}), f32[8,128,32]{1,2,0:T(8,128)S(1)}, u32[]{:S(2)}, u32[]{:S(2)}) %all-to-all-start.2) | async-done | bytes 131104 | tf_op jit(solution)/shard_map/all_to_all | solution.py:15
  81.4 0.1 fusion.45
  81.6 0.1 pad_maximum_fusion.4
  81.7 0.3 fusion.16
  82.0 1.0 pad_maximum_fusion
  83.0 5.5 %all-to-all-start.3 = ((f32[64,16,96]{2,1,0:T(8,128)}), f32[64,16,96]{2,1,0:T(8,128)}, u32[]{:S(2)}, u32[]{:S(2)}) async-start(f32[64,16,96]{2,1,0:T(8,128)} %pad_maximum_fusion), calls=%async_computation.3 | async-start | bytes 1048576 | tf_op jit(solution)/shard_map/all_to_all | solution.py:15
  88.5 0.4 fusion.3
  88.9 15.2 %all-to-all-done.3 = f32[64,16,96]{2,1,0:T(8,128)} async-done(((f32[64,16,96]{2,1,0:T(8,128)}), f32[64,16,96]{2,1,0:T(8,128)}, u32[]{:S(2)}, u32[]{:S(2)}) %all-to-all-start.3) | async-done | bytes 393248 | tf_op jit(solution)/shard_map/all_to_all | solution.py:15
  104.1 1.1 reduce_sum.37
  105.2 0.1 reduce-precision_convert_fusion.3
  105.3 0.5 convolution_add_fusion.2
  105.7 0.1 slice_add_fusion
  105.8 0.4 reshape.67
  106.3 1.6 copy.34
  107.8 6.8 %all-to-all-start.4 = ((f32[64,32,96]{2,1,0:T(8,128)}), f32[64,32,96]{2,1,0:T(8,128)S(1)}, u32[]{:S(2)}, u32[]{:S(2)}) async-start(f32[64,32,96]{2,1,0:T(8,128)} %bitcast.70), calls=%async_computation.4 | async-start | bytes 2097152 | tf_op jit(solution)/shard_map/all_to_all | solution.py:15
  114.7 0.1 copy.31
  114.8 0.1 copy.32
  114.8 0.1 pad_maximum_fusion.2
  114.9 0.1 copy.26
  115.0 0.1 fusion.40
  115.1 2.9 %cholesky.17 = f32[32,32]{1,0:T(8,128)S(1)} custom-call(f32[32,32]{1,0:T(8,128)S(1)} %fusion.40), custom_call_target="Cholesky" | custom-call | tf_op jit(solution)/shard_map/jit(cholesky)/cholesky | solution.py:92
  118.0 0.6 compare_reduce_fusion
  118.7 0.7 fusion.24
  119.3 2.4 %custom-call.6 = f32[1,32,32]{1,2,0:T(8,128)S(1)} custom-call(f32[1,32,32]{2,1,0:T(8,128)S(1)} %fusion.24), custom_call_target="InvertDiagBlocksLowerTriangular" | custom-call | tf_op jit(solution)/shard_map/triangular_solve | solution.py:93
  121.8 30.1 %all-to-all-done.4 = f32[64,32,96]{2,1,0:T(8,128)S(1)} async-done(((f32[64,32,96]{2,1,0:T(8,128)}), f32[64,32,96]{2,1,0:T(8,128)S(1)}, u32[]{:S(2)}, u32[]{:S(2)}) %all-to-all-start.4) | async-done | bytes 786464 | tf_op jit(solution)/shard_map/all_to_all | solution.py:15
  151.9 0.1 reduce_sum.38
  152.0 0.7 broadcast_in_dim.22
  152.6 7.4 %all-to-all-start.5 = ((f32[8,32,96]{2,1,0:T(8,128)}), f32[8,32,96]{2,1,0:T(8,128)S(1)}, u32[]{:S(2)}, u32[]{:S(2)}) async-start(f32[8,32,96]{2,1,0:T(8,128)} %broadcast_in_dim.22), calls=%async_computation.5 | async-start | bytes 262144 | tf_op jit(solution)/shard_map/all_to_all | solution.py:15
  160.1 0.2 fusion.38
  160.2 7.8 %all-to-all-done.5 = f32[8,32,96]{2,1,0:T(8,128)S(1)} async-done(((f32[8,32,96]{2,1,0:T(8,128)}), f32[8,32,96]{2,1,0:T(8,128)S(1)}, u32[]{:S(2)}, u32[]{:S(2)}) %all-to-all-start.5) | async-done | bytes 98336 | tf_op jit(solution)/shard_map/all_to_all | solution.py:15
  168.1 0.8 reduce-precision_convert_fusion.1
  168.9 1.2 broadcast_in_dim.24
  170.1 6.2 %all-to-all-start.6 = ((bf16[64,64,96]{2,1,0:T(8,128)(2,1)}), bf16[64,64,96]{2,1,0:T(8,128)(2,1)S(1)}, u32[]{:S(2)}, u32[]{:S(2)}) async-start(bf16[64,64,96]{2,1,0:T(8,128)(2,1)} %broadcast_in_dim.24), calls=%async_computation.6 | async-start | bytes 2097152 | tf_op jit(solution)/shard_map/all_to_all | solution.py:15
  176.4 0.1 reduce-precision_convert_fusion
  176.5 21.5 %all-gather.2.cloned.1.call-done = bf16[1024,6144]{1,0:T(8,128)(2,1)} async-done(((bf16[32,6144]{1,0:T(8,128)(2,1)}), bf16[1024,6144]{1,0:T(8,128)(2,1)}) %all-gather.2.cloned.1.call-update) | async-done | bytes 12582928 | tf_op jit(solution)/shard_map/all_gather | solution.py:52
  198.0 8.1 %convolution_add_fusion.1 = f32[128,6144]{1,0:T(8,128)} fusion(bf16[1024,128]{1,0:T(8,128)(2,1)S(1)} %bitcast.74, bf16[1024,6144]{1,0:T(8,128)(2,1)} %all-gather.2.cloned.1.call-done, bf16[1,128,6144]{2,1,0:T(8,128)(2,1)S(1)} %copy-done), kind=kOutput, calls=%fused_computation.2 | convolution fusion | flops 1612185600 | bytes 17563648 | tf_op jit(solution)/shard_map/dot_general | solution.py:28
  206.1 2.9 %all-to-all-done.6 = bf16[64,64,96]{2,1,0:T(8,128)(2,1)S(1)} async-done(((bf16[64,64,96]{2,1,0:T(8,128)(2,1)}), bf16[64,64,96]{2,1,0:T(8,128)(2,1)S(1)}, u32[]{:S(2)}, u32[]{:S(2)}) %all-to-all-start.6) | async-done | bytes 786464 | tf_op jit(solution)/shard_map/all_to_all | solution.py:15
  209.0 0.7 copy.28
  209.7 1.4 reshape.68
  211.2 0.2 copy.29
  211.4 0.7 slice.65
  212.1 0.6 fusion.34
  212.7 1.3 copy-done.1
  214.0 1.8 fusion.2
  (27 shorter events, 0.3 us)
Async XLA Ops:
  7.2 16.9 %copy-start.2 = (bf16[1,16,6144]{2,1,0:T(8,128)(2,1)S(1)}, bf16[1,16,6144]{2,1,0:T(8,128)(2,1)}, u32[]{:S(2)}) copy-start(bf16[1,16,6144]{2,1,0:T(8,128)(2,1)} %param.7) | copy-start | bytes 589828
  7.2 16.9 %collective-permute-start = (bf16[16,6144]{1,0:T(8,128)(2,1)}, bf16[16,6144]{1,0:T(8,128)(2,1)S(1)}, u32[]{:S(2)}, u32[]{:S(2)}) collective-permute-start(bf16[16,6144]{1,0:T(8,128)(2,1)} %bitcast.72), channel_id=1, source_target_pairs={{0,32},{32,0},{1,33},{33,1},{2,34},{34,2},{3,35},{35,3},{4,36},{36... | collective-permute-start | bytes 589832 | tf_op jit(solution)/shard_map/ppermute | solution.py:49
  13.7 26.0 %all-to-all-start = ((bf16[64,32,96]{2,1,0:T(8,128)(2,1)}), bf16[64,32,96]{2,1,0:T(8,128)(2,1)S(1)}, u32[]{:S(2)}, u32[]{:S(2)}) async-start(bf16[64,32,96]{2,1,0:T(8,128)(2,1)} %broadcast_in_dim.18), calls=%async_computation | async-start | bytes 1048576 | tf_op jit(solution)/shard_map/all_to_all | solution.py:15
  24.0 174.0 %all-gather.2.cloned.1.call-start = ((), (), s32[]{:S(2)}) async-start(), calls=%async_computation.7 | async-start | bytes 12976128 | tf_op jit(solution)/shard_map/all_gather | solution.py:52
  39.8 9.6 %copy-start.6 = (f32[1,1024]{1,0:T(1,128)S(1)}, f32[1,1024]{1,0:T(1,128)}, u32[]{:S(2)}) copy-start(f32[1,1024]{1,0:T(1,128)} %param.8) | copy-start | bytes 12292
  40.0 19.0 %copy-start.5 = (bf16[1,1024,128]{2,1,0:T(8,128)(2,1)S(1)}, bf16[1,1024,128]{2,1,0:T(8,128)(2,1)}, u32[]{:S(2)}) copy-start(bf16[1,1024,128]{2,1,0:T(8,128)(2,1)} %param.6) | copy-start | bytes 786436
  40.0 19.4 %copy-start = (bf16[1,128,6144]{2,1,0:T(8,128)(2,1)S(1)}, bf16[1,128,6144]{2,1,0:T(8,128)(2,1)}, u32[]{:S(2)}) copy-start(bf16[1,128,6144]{2,1,0:T(8,128)(2,1)} %param.10) | copy-start | bytes 4718596
  41.9 16.8 %all-to-all-start.1 = ((bf16[64,2,512]{2,1,0:T(2,128)(2,1)}), bf16[64,2,512]{2,1,0:T(2,128)(2,1)S(1)}, u32[]{:S(2)}, u32[]{:S(2)}) async-start(bf16[64,2,512]{2,1,0:T(2,128)(2,1)} %reshape.70), calls=%async_computation.1 | async-start | bytes 262144 | tf_op jit(solution)/shard_map/all_to_all | solution.py:15
  60.7 20.7 %all-to-all-start.2 = ((f32[8,128,32]{1,2,0:T(8,128)}), f32[8,128,32]{1,2,0:T(8,128)S(1)}, u32[]{:S(2)}, u32[]{:S(2)}) async-start(f32[8,128,32]{1,2,0:T(8,128)} %broadcast_in_dim.20), calls=%async_computation.2 | async-start | bytes 262144 | tf_op jit(solution)/shard_map/all_to_all | solution.py:15
  73.6 9.4 %copy-start.3 = (bf16[1024,128]{1,0:T(8,128)(2,1)}, bf16[1024,128]{1,0:T(8,128)(2,1)S(1)}, u32[]{:S(2)}) copy-start(bf16[1024,128]{1,0:T(8,128)(2,1)S(1)} %fusion.14) | copy-start | bytes 786436
  83.0 21.1 %all-to-all-start.3 = ((f32[64,16,96]{2,1,0:T(8,128)}), f32[64,16,96]{2,1,0:T(8,128)}, u32[]{:S(2)}, u32[]{:S(2)}) async-start(f32[64,16,96]{2,1,0:T(8,128)} %pad_maximum_fusion), calls=%async_computation.3 | async-start | bytes 1048576 | tf_op jit(solution)/shard_map/all_to_all | solution.py:15
  107.8 44.0 %all-to-all-start.4 = ((f32[64,32,96]{2,1,0:T(8,128)}), f32[64,32,96]{2,1,0:T(8,128)S(1)}, u32[]{:S(2)}, u32[]{:S(2)}) async-start(f32[64,32,96]{2,1,0:T(8,128)} %bitcast.70), calls=%async_computation.4 | async-start | bytes 2097152 | tf_op jit(solution)/shard_map/all_to_all | solution.py:15
  152.6 15.4 %all-to-all-start.5 = ((f32[8,32,96]{2,1,0:T(8,128)}), f32[8,32,96]{2,1,0:T(8,128)S(1)}, u32[]{:S(2)}, u32[]{:S(2)}) async-start(f32[8,32,96]{2,1,0:T(8,128)} %broadcast_in_dim.22), calls=%async_computation.5 | async-start | bytes 262144 | tf_op jit(solution)/shard_map/all_to_all | solution.py:15
  168.9 7.4 %copy-start.4 = (bf16[1024,128]{1,0:T(8,128)(2,1)S(1)}, bf16[1024,128]{1,0:T(8,128)(2,1)}, u32[]{:S(2)}) copy-start(bf16[1024,128]{1,0:T(8,128)(2,1)} %copy-done.3) | copy-start | bytes 786436
  170.1 38.9 %all-to-all-start.6 = ((bf16[64,64,96]{2,1,0:T(8,128)(2,1)}), bf16[64,64,96]{2,1,0:T(8,128)(2,1)S(1)}, u32[]{:S(2)}, u32[]{:S(2)}) async-start(bf16[64,64,96]{2,1,0:T(8,128)(2,1)} %broadcast_in_dim.24), calls=%async_computation.6 | async-start | bytes 2097152 | tf_op jit(solution)/shard_map/all_to_all | solution.py:15
  212.1 1.9 copy-start.1
Sparse Core Ops, SparseCore 0:
  39.9 158.0 all-gather.1

commit v3 on v2

--- a/solution.py
+++ b/solution.py
@@ -17,6 +17,10 @@
 
 def spread(block, axes, count):
     return exchange(jnp.broadcast_to(block[None], (count,) + block.shape), axes)
+
+
+def swap(values):
+    return lax.ppermute(values, "zl", [(0, 1), (1, 0)])
 
 
 def halves(values):
@@ -46,20 +50,27 @@
 
     query_low = old_query.astype(bf16)
     query_blocks = spread(query_low.T, DP, members)
-    partner_rows = lax.ppermute(grad_rows, "zl", [(0, 1), (1, 0)])
-    pair_rows = jnp.concatenate([grad_rows, partner_rows], axis=0)
-    query_blocks, pair_rows = lax.optimization_barrier((query_blocks, pair_rows))
-    full_grad = lax.all_gather(pair_rows, PLANE, axis=0, tiled=True)
-    full_query = query_blocks.transpose(1, 0, 2).reshape(rank, width)
-
     live_slots = lax.iota(jnp.int32, slots) < counts[0]
     slot_scale = jnp.where(live_slots, gate_weight[0], jnp.zeros_like(gate_weight[0]))
     weighted = (hidden_local.astype(f32) * slot_scale[:, None]).astype(bf16)
 
+    own_first = lax.axis_index("zl") == 0
+    half = width // 2
+    left_cols, right_cols = grad_rows[:, :half], grad_rows[:, half:]
+    kept_rows = jnp.where(own_first, left_cols, right_cols)
+    partner_rows = swap(jnp.where(own_first, right_cols, left_cols))
+    pair_rows = jnp.concatenate([kept_rows, partner_rows], axis=0)
+    query_blocks, pair_rows = lax.optimization_barrier((query_blocks, pair_rows))
+    half_grad = lax.all_gather(pair_rows, PLANE, axis=0, tiled=True)
+    pair_weighted = jnp.concatenate([weighted, swap(weighted)], axis=1)
+    full_query = query_blocks.transpose(1, 0, 2).reshape(rank, width)
+
     slot_query = product(grad_rows, full_query, 1, 1)
-    slot_pair = spread(jnp.concatenate(halves(slot_query), axis=1), DP, members).reshape(slots, 2 * rank)
-    left_pair = product(weighted, slot_pair, 0, 0)
-    left_part = left_pair[:, :rank] + left_pair[:, rank:] + product(error_local, full_query, 1, 1)
+    slot_high, slot_low = halves(slot_query)
+    slot_wide = jnp.concatenate([slot_high, slot_low, jnp.zeros((own_slots, 2 * rank), bf16)], axis=1)
+    all_slots = spread(slot_wide, DP, members).reshape(slots, 4 * rank)
+    left_pair = product(weighted, all_slots, 0, 0)
+    left_part = left_pair[:, :rank] + left_pair[:, rank : 2 * rank] + product(error_local, full_query, 1, 1)
     left_sum = jnp.sum(spread(left_part, EXPERT, replicas), axis=0) / replicas
 
     sum_high, sum_low = halves(left_sum)
@@ -100,20 +111,30 @@
     new_rows = new_cols.T
     col_blocks = spread(jnp.concatenate(halves(new_cols), axis=0), DP, members)
 
-    own_first = lax.axis_index("zl") == 0
-    parts = weighted.reshape(2, plane, own_slots, units)
+    parts = pair_weighted.reshape(2, plane, own_slots, 2 * units)
     ordered = jnp.where(
         own_first,
         jnp.stack([parts[0], parts[1]], axis=1),
         jnp.stack([parts[1], parts[0]], axis=1),
-    ).reshape(slots, units)
-    merged = product(ordered, full_grad, 0, 0) + error_local.astype(f32)
+    ).reshape(slots, 2 * units)
+    both_grad = product(ordered, half_grad, 0, 0)
+    kept_grad, sent_grad = both_grad[:units], swap(both_grad[units:])
+    merged = (
+        jnp.concatenate(
+            [
+                jnp.where(own_first, kept_grad, sent_grad),
+                jnp.where(own_first, sent_grad, kept_grad),
+            ],
+            axis=1,
+        )
+        + error_local.astype(f32)
+    )
     merged, col_blocks = lax.optimization_barrier((merged, col_blocks))
     col_pair = col_blocks.transpose(1, 0, 2).reshape(2 * rank, width)
     basis_high, basis_low = halves(left_basis)
     correction = product(
         jnp.concatenate([basis_high, basis_high], axis=1), col_pair, 1, 0
-    ) + product(basis_low, col_pair[:rank], 1, 0)
+    ) + product(jnp.concatenate([basis_low, jnp.zeros_like(basis_low)], axis=1), col_pair, 1, 0)
     new_error = (merged - correction).astype(bf16)
     return (new_error[None], new_rows)
 

time: 226 us -> 258 us (1.14)
  waiting for transfers between devices: 110 us -> 130 us
  starting transfers between devices: 60.7 us -> 69.9 us
  other arithmetic: 11.2 us -> 16.2 us
  matrix products: 14 us -> 10.7 us
    all_gather x1, waiting for transfers between devices: 21.5 us -> 41 us  [body(): half_grad = lax.all_gather(pair_rows, PLANE, axis=0, tiled=True)]
    all_to_all x7, starting transfers between devices: 55.7 us -> 61.9 us  [exchange(): return lax.all_to_all(blocks, axes, split_axis=0, concat_axis=0, tiled=True)]
    ppermute x1 -> x3, waiting for transfers between devices: 0.01 us -> 4.7 us  [swap(): return lax.ppermute(values, 'zl', [(0, 1), (1, 0)])]
    all_to_all x7, waiting for transfers between devices: 88 us -> 84.6 us  [exchange(): return lax.all_to_all(blocks, axes, split_axis=0, concat_axis=0, tiled=True)]
    dot_general x9, matrix products: 12.8 us -> 9.42 us  [product(): lax.dot_general(left_side, right_side, (((left_dim,), (right_dim,)), ((),...]
    ppermute x1 -> x3, starting transfers between devices: 4.96 us -> 7.98 us  [swap(): return lax.ppermute(values, 'zl', [(0, 1), (1, 0)])]
  transfers between devices with their start and end apart: 9 -> 11, of which waited for: 8 -> 8; matrix products, arithmetic and copies ran while one was open for 14% -> 12% of each run, Pallas kernels for 0% -> 0%
where the time goes in v3:
time: 258 us; the launch traced here: 255 us
  waiting for transfers between devices  130 us (50%)
  starting transfers between devices  69.9 us (27%)
  other arithmetic  16.2 us (6%)
  between operations  15 us (6%)
  local copies, waits for them, and re-layouts  13.1 us (5%)
  matrix products  10.7 us (4%)
    all_to_all x7, waiting for transfers between devices, exchange(): return lax.all_to_all(blocks, axes, split_axis=0, concat_axis=0, tiled=True)  84.6 us
    all_to_all x7, starting transfers between devices, exchange(): return lax.all_to_all(blocks, axes, split_axis=0, concat_axis=0, tiled=True)  61.9 us
    all_gather x1, waiting for transfers between devices, body(): half_grad = lax.all_gather(pair_rows, PLANE, axis=0, tiled=True)  41 us
    dot_general x9, matrix products, product(): lax.dot_general(left_side, right_side, (((left_dim,), (right_dim,)), ((),...  9.42 us
    ppermute x3, starting transfers between devices, swap(): return lax.ppermute(values, 'zl', [(0, 1), (1, 0)])  7.98 us
  transfers between devices with their start and end apart: 11, of which 8 were waited for; matrix products, arithmetic and copies ran while one was open for 12% of the time, Pallas kernels for 0%

profile of v3, /device:TPU:1, one launch (start us, length us, event | category | flops | bytes accessed | tf_op | source)
XLA Modules:
  0.0 255.1 jit_solution(14007657456070112270)
XLA Ops:
  7.2 0.8 convert_bitcast_fusion.1
  7.9 0.9 broadcast_in_dim.20
  8.8 12.9 %all-to-all-start = ((bf16[64,32,96]{2,1,0:T(8,128)(2,1)}), bf16[64,32,96]{2,1,0:T(8,128)(2,1)S(1)}, u32[]{:S(2)}, u32[]{:S(2)}) async-start(bf16[64,32,96]{2,1,0:T(8,128)(2,1)} %broadcast_in_dim.20), calls=%async_computation | async-start | bytes 1048576 | tf_op jit(solution)/shard_map/all_to_all | solution.py:15
  21.8 3.0 %collective-permute-start.1 = (bf16[16,3072]{1,0:T(8,128)(2,1)S(1)}, bf16[16,3072]{1,0:T(8,128)(2,1)S(1)}, u32[]{:S(2)}, u32[]{:S(2)}) collective-permute-start(bf16[16,3072]{1,0:T(8,128)(2,1)S(1)} %get-tuple-element.15), channel_id=1, source_target_pairs={{0,32},{32,0},{1,33},{33,1},{2,34},{34,2},{3,35},{35,3},{4,36},{36... | collective-permute-start | bytes 294920 | tf_op jit(solution)/shard_map/ppermute | solution.py:23
  24.9 4.7 %collective-permute-done.1 = bf16[16,3072]{1,0:T(8,128)(2,1)S(1)} collective-permute-done((bf16[16,3072]{1,0:T(8,128)(2,1)S(1)}, bf16[16,3072]{1,0:T(8,128)(2,1)S(1)}, u32[]{:S(2)}, u32[]{:S(2)}) %collective-permute-start.1) | collective-permute-done | bytes 98336 | tf_op jit(solution)/shard_map/ppermute | solution.py:23
  29.5 0.7 pad_maximum_fusion.4
  30.2 7.4 %all-to-all-done = bf16[64,32,96]{2,1,0:T(8,128)(2,1)S(1)} async-done(((bf16[64,32,96]{2,1,0:T(8,128)(2,1)}), bf16[64,32,96]{2,1,0:T(8,128)(2,1)S(1)}, u32[]{:S(2)}, u32[]{:S(2)}) %all-to-all-start) | async-done | bytes 393248 | tf_op jit(solution)/shard_map/all_to_all | solution.py:15
  37.7 0.1 pad.19.clone
  37.8 0.2 copy.21
  38.0 0.7 reshape.63
  38.7 0.2 reduce-precision_convert_fusion.4
  39.0 0.1 maximum_maximum_fusion
  39.1 0.8 broadcast_in_dim.22
  39.8 6.9 %all-to-all-start.1 = ((bf16[64,16,128]{2,1,0:T(8,128)(2,1)}), bf16[64,16,128]{2,1,0:T(8,128)(2,1)S(1)}, u32[]{:S(2)}, u32[]{:S(2)}) async-start(bf16[64,16,128]{2,1,0:T(8,128)(2,1)} %broadcast_in_dim.22), calls=%async_computation.1 | async-start | bytes 524288 | tf_op jit(solution)/shard_map/all_to_all | solution.py:15
  47.4 10.0 %all-to-all-done.1 = bf16[64,16,128]{2,1,0:T(8,128)(2,1)S(1)} async-done(((bf16[64,16,128]{2,1,0:T(8,128)(2,1)}), bf16[64,16,128]{2,1,0:T(8,128)(2,1)S(1)}, u32[]{:S(2)}, u32[]{:S(2)}) %all-to-all-start.1) | async-done | bytes 262176 | tf_op jit(solution)/shard_map/all_to_all | solution.py:15
  57.4 0.4 fusion.20
  57.9 0.6 fusion.10
  58.5 0.7 broadcast_in_dim.23
  59.2 13.1 %all-to-all-start.2 = ((f32[8,128,32]{1,2,0:T(8,128)}), f32[8,128,32]{1,2,0:T(8,128)S(1)}, u32[]{:S(2)}, u32[]{:S(2)}) async-start(f32[8,128,32]{1,2,0:T(8,128)} %broadcast_in_dim.23), calls=%async_computation.2 | async-start | bytes 262144 | tf_op jit(solution)/shard_map/all_to_all | solution.py:15
  72.3 0.2 fusion.15
  72.5 1.9 collective-permute-start
  74.4 5.9 %all-to-all-done.2 = f32[8,128,32]{1,2,0:T(8,128)S(1)} async-done(((f32[8,128,32]{1,2,0:T(8,128)}), f32[8,128,32]{1,2,0:T(8,128)S(1)}, u32[]{:S(2)}, u32[]{:S(2)}) %all-to-all-start.2) | async-done | bytes 131104 | tf_op jit(solution)/shard_map/all_to_all | solution.py:15
  80.4 0.1 fusion.45
  80.5 0.1 pad_maximum_fusion.7
  80.6 0.3 fusion.13
  80.9 1.0 pad_maximum_fusion.2
  81.9 5.8 %all-to-all-start.3 = ((f32[64,16,96]{2,1,0:T(8,128)}), f32[64,16,96]{2,1,0:T(8,128)}, u32[]{:S(2)}, u32[]{:S(2)}) async-start(f32[64,16,96]{2,1,0:T(8,128)} %pad_maximum_fusion.2), calls=%async_computation.3 | async-start | bytes 1048576 | tf_op jit(solution)/shard_map/all_to_all | solution.py:15
  87.8 0.8 maximum_select_fusion
  88.7 0.4 fusion.3
  89.1 13.3 %all-to-all-done.3 = f32[64,16,96]{2,1,0:T(8,128)} async-done(((f32[64,16,96]{2,1,0:T(8,128)}), f32[64,16,96]{2,1,0:T(8,128)}, u32[]{:S(2)}, u32[]{:S(2)}) %all-to-all-start.3) | async-done | bytes 393248 | tf_op jit(solution)/shard_map/all_to_all | solution.py:15
  102.4 1.1 reduce_sum.37
  103.7 0.5 convolution_add_fusion.1
  104.2 0.1 slice_add_fusion
  104.3 0.4 reshape.66
  104.7 1.6 copy.32
  106.3 8.8 %all-to-all-start.4 = ((f32[64,32,96]{2,1,0:T(8,128)}), f32[64,32,96]{2,1,0:T(8,128)S(1)}, u32[]{:S(2)}, u32[]{:S(2)}) async-start(f32[64,32,96]{2,1,0:T(8,128)} %bitcast.68), calls=%async_computation.4 | async-start | bytes 2097152 | tf_op jit(solution)/shard_map/all_to_all | solution.py:15
  115.1 41.0 %all-gather.2.cloned.1.call-done = bf16[1024,3072]{1,0:T(8,128)(2,1)} async-done(((bf16[32,3072]{1,0:T(8,128)(2,1)}), bf16[1024,3072]{1,0:T(8,128)(2,1)}) %all-gather.2.cloned.1.call-update) | async-done | bytes 6291472 | tf_op jit(solution)/shard_map/all_gather | solution.py:64
  156.0 4.7 %fusion.67 = f32[256,3072]{1,0:T(8,128)S(1)} fusion(bf16[1024,256]{1,0:T(8,128)(2,1)S(1)} %bitcast.70, bf16[1024,3072]{1,0:T(8,128)(2,1)} %all-gather.2.cloned.1.call-done), kind=kOutput, calls=%fused_computation.104 | convolution fusion | flops 1610612736 | bytes 9961472 | tf_op jit(solution)/shard_map/dot_general | solution.py:32
  160.7 1.3 slice.79
  162.1 0.8 copy-done.2
  162.9 3.0 %collective-permute-start.2 = (f32[128,3072]{1,0:T(8,128)}, f32[128,3072]{1,0:T(8,128)}, u32[]{:S(2)}, u32[]{:S(2)}) collective-permute-start(f32[128,3072]{1,0:T(8,128)} %slice.79), channel_id=1, source_target_pairs={{0,32},{32,0},{1,33},{33,1},{2,34},{34,2},{3,35},{35,3},{4,36},{36... | collective-permute-start | bytes 4718600 | tf_op jit(solution)/shard_map/ppermute | solution.py:23
  165.9 0.1 pad_maximum_fusion.5
  166.1 0.1 fusion.39
  166.2 2.9 %cholesky.17 = f32[32,32]{1,0:T(8,128)S(1)} custom-call(f32[32,32]{1,0:T(8,128)S(1)} %fusion.39), custom_call_target="Cholesky" | custom-call | tf_op jit(solution)/shard_map/jit(cholesky)/cholesky | solution.py:103
  169.1 0.6 compare_reduce_fusion
  169.8 0.7 fusion.23
  170.4 2.4 custom-call.6
  172.9 0.2 fusion.37
  173.1 0.1 reduce_sum.38
  173.2 0.7 broadcast_in_dim.26
  173.9 7.1 %all-to-all-start.5 = ((f32[8,32,96]{2,1,0:T(8,128)}), f32[8,32,96]{2,1,0:T(8,128)S(1)}, u32[]{:S(2)}, u32[]{:S(2)}) async-start(f32[8,32,96]{2,1,0:T(8,128)} %broadcast_in_dim.26), calls=%async_computation.5 | async-start | bytes 262144 | tf_op jit(solution)/shard_map/all_to_all | solution.py:15
  181.0 0.1 fusion.26
  181.1 25.6 %all-to-all-done.5 = f32[8,32,96]{2,1,0:T(8,128)S(1)} async-done(((f32[8,32,96]{2,1,0:T(8,128)}), f32[8,32,96]{2,1,0:T(8,128)S(1)}, u32[]{:S(2)}, u32[]{:S(2)}) %all-to-all-start.5) | async-done | bytes 98336 | tf_op jit(solution)/shard_map/all_to_all | solution.py:15
  206.7 0.8 reduce-precision_convert_fusion.1
  207.4 1.2 broadcast_in_dim.27
  208.7 7.3 %all-to-all-start.6 = ((bf16[64,64,96]{2,1,0:T(8,128)(2,1)}), bf16[64,64,96]{2,1,0:T(8,128)(2,1)S(1)}, u32[]{:S(2)}, u32[]{:S(2)}) async-start(bf16[64,64,96]{2,1,0:T(8,128)(2,1)} %broadcast_in_dim.27), calls=%async_computation.6 | async-start | bytes 2097152 | tf_op jit(solution)/shard_map/all_to_all | solution.py:15
  216.0 2.2 slice_select_fusion.1
  218.2 2.0 maximum_add_fusion
  220.2 22.3 %all-to-all-done.6 = bf16[64,64,96]{2,1,0:T(8,128)(2,1)S(1)} async-done(((bf16[64,64,96]{2,1,0:T(8,128)(2,1)}), bf16[64,64,96]{2,1,0:T(8,128)(2,1)S(1)}, u32[]{:S(2)}, u32[]{:S(2)}) %all-to-all-start.6) | async-done | bytes 786464 | tf_op jit(solution)/shard_map/all_to_all | solution.py:15
  242.5 0.7 copy.27
  243.2 1.4 reshape.67
  244.6 0.6 fusion.33
  245.2 1.3 copy-done.1
  246.5 1.8 fusion.2
  (32 shorter events, 0.6 us)
Async XLA Ops:
  7.2 14.6 %copy-start.4 = (bf16[1,16,6144]{2,1,0:T(8,128)(2,1)S(1)}, bf16[1,16,6144]{2,1,0:T(8,128)(2,1)}, u32[]{:S(2)}) copy-start(bf16[1,16,6144]{2,1,0:T(8,128)(2,1)} %param.7) | copy-start | bytes 589828
  8.8 28.9 %all-to-all-start = ((bf16[64,32,96]{2,1,0:T(8,128)(2,1)}), bf16[64,32,96]{2,1,0:T(8,128)(2,1)S(1)}, u32[]{:S(2)}, u32[]{:S(2)}) async-start(bf16[64,32,96]{2,1,0:T(8,128)(2,1)} %broadcast_in_dim.20), calls=%async_computation | async-start | bytes 1048576 | tf_op jit(solution)/shard_map/all_to_all | solution.py:15
  21.7 134.3 %all-gather.2.cloned.1.call-start = ((), (), s32[]{:S(2)}) async-start(), calls=%async_computation.7 | async-start | bytes 6488064 | tf_op jit(solution)/shard_map/all_gather | solution.py:64
  21.8 7.7 %collective-permute-start.1 = (bf16[16,3072]{1,0:T(8,128)(2,1)S(1)}, bf16[16,3072]{1,0:T(8,128)(2,1)S(1)}, u32[]{:S(2)}, u32[]{:S(2)}) collective-permute-start(bf16[16,3072]{1,0:T(8,128)(2,1)S(1)} %get-tuple-element.15), channel_id=1, source_target_pairs={{0,32},{32,0},{1,33},{33,1},{2,34},{34,2},{3,35},{35,3},{4,36},{36... | collective-permute-start | bytes 294920 | tf_op jit(solution)/shard_map/ppermute | solution.py:23
  37.8 9.6 %copy-start.6 = (f32[1,1024]{1,0:T(1,128)S(1)}, f32[1,1024]{1,0:T(1,128)}, u32[]{:S(2)}) copy-start(f32[1,1024]{1,0:T(1,128)} %param.8) | copy-start | bytes 12292
  37.8 19.6 %copy-start.5 = (bf16[1,1024,128]{2,1,0:T(8,128)(2,1)S(1)}, bf16[1,1024,128]{2,1,0:T(8,128)(2,1)}, u32[]{:S(2)}) copy-start(bf16[1,1024,128]{2,1,0:T(8,128)(2,1)} %param.6) | copy-start | bytes 786436
  38.0 19.9 %copy-start = (bf16[1,128,6144]{2,1,0:T(8,128)(2,1)S(1)}, bf16[1,128,6144]{2,1,0:T(8,128)(2,1)}, u32[]{:S(2)}) copy-start(bf16[1,128,6144]{2,1,0:T(8,128)(2,1)} %param.10) | copy-start | bytes 4718596
  39.8 17.6 %all-to-all-start.1 = ((bf16[64,16,128]{2,1,0:T(8,128)(2,1)}), bf16[64,16,128]{2,1,0:T(8,128)(2,1)S(1)}, u32[]{:S(2)}, u32[]{:S(2)}) async-start(bf16[64,16,128]{2,1,0:T(8,128)(2,1)} %broadcast_in_dim.22), calls=%async_computation.1 | async-start | bytes 524288 | tf_op jit(solution)/shard_map/all_to_all | solution.py:15
  59.2 21.2 %all-to-all-start.2 = ((f32[8,128,32]{1,2,0:T(8,128)}), f32[8,128,32]{1,2,0:T(8,128)S(1)}, u32[]{:S(2)}, u32[]{:S(2)}) async-start(f32[8,128,32]{1,2,0:T(8,128)} %broadcast_in_dim.23), calls=%async_computation.2 | async-start | bytes 262144 | tf_op jit(solution)/shard_map/all_to_all | solution.py:15
  72.5 15.3 %collective-permute-start = (bf16[1024,128]{1,0:T(8,128)(2,1)S(1)}, bf16[1024,128]{1,0:T(8,128)(2,1)S(1)}, u32[]{:S(2)}, u32[]{:S(2)}) collective-permute-start(bf16[1024,128]{1,0:T(8,128)(2,1)S(1)} %fusion.15), channel_id=1, source_target_pairs={{0,32},{32,0},{1,33},{33,1},{2,34},{34,2},{3,35},{35,3},{4,36},{36... | collective-permute-start | bytes 786440 | tf_op jit(solution)/shard_map/ppermute | solution.py:23
  81.9 20.4 %all-to-all-start.3 = ((f32[64,16,96]{2,1,0:T(8,128)}), f32[64,16,96]{2,1,0:T(8,128)}, u32[]{:S(2)}, u32[]{:S(2)}) async-start(f32[64,16,96]{2,1,0:T(8,128)} %pad_maximum_fusion.2), calls=%async_computation.3 | async-start | bytes 1048576 | tf_op jit(solution)/shard_map/all_to_all | solution.py:15
  106.3 49.7 %copy-start.3 = (bf16[32,2,16,256]{3,2,1,0:T(8,128)(2,1)S(1)}, bf16[32,2,16,256]{3,2,1,0:T(8,128)(2,1)}, u32[]{:S(2)}) copy-start(bf16[32,2,16,256]{3,2,1,0:T(8,128)(2,1)} %maximum_select_fusion) | copy-start | bytes 1572868
  106.3 66.8 %all-to-all-start.4 = ((f32[64,32,96]{2,1,0:T(8,128)}), f32[64,32,96]{2,1,0:T(8,128)S(1)}, u32[]{:S(2)}, u32[]{:S(2)}) async-start(f32[64,32,96]{2,1,0:T(8,128)} %bitcast.68), calls=%async_computation.4 | async-start | bytes 2097152 | tf_op jit(solution)/shard_map/all_to_all | solution.py:15
  160.7 2.2 copy-start.2
  162.9 53.1 %collective-permute-start.2 = (f32[128,3072]{1,0:T(8,128)}, f32[128,3072]{1,0:T(8,128)}, u32[]{:S(2)}, u32[]{:S(2)}) collective-permute-start(f32[128,3072]{1,0:T(8,128)} %slice.79), channel_id=1, source_target_pairs={{0,32},{32,0},{1,33},{33,1},{2,34},{34,2},{3,35},{35,3},{4,36},{36... | collective-permute-start | bytes 4718600 | tf_op jit(solution)/shard_map/ppermute | solution.py:23
  173.9 32.8 %all-to-all-start.5 = ((f32[8,32,96]{2,1,0:T(8,128)}), f32[8,32,96]{2,1,0:T(8,128)S(1)}, u32[]{:S(2)}, u32[]{:S(2)}) async-start(f32[8,32,96]{2,1,0:T(8,128)} %broadcast_in_dim.26), calls=%async_computation.5 | async-start | bytes 262144 | tf_op jit(solution)/shard_map/all_to_all | solution.py:15
  208.7 33.8 %all-to-all-start.6 = ((bf16[64,64,96]{2,1,0:T(8,128)(2,1)}), bf16[64,64,96]{2,1,0:T(8,128)(2,1)S(1)}, u32[]{:S(2)}, u32[]{:S(2)}) async-start(bf16[64,64,96]{2,1,0:T(8,128)(2,1)} %broadcast_in_dim.27), calls=%async_computation.6 | async-start | bytes 2097152 | tf_op jit(solution)/shard_map/all_to_all | solution.py:15
  244.6 1.9 copy-start.1
Sparse Core Ops, SparseCore 0:
  37.8 118.1 all-gather.1

commit v4 on v2

--- a/solution.py
+++ b/solution.py
@@ -17,6 +17,14 @@
 
 def spread(block, axes, count):
     return exchange(jnp.broadcast_to(block[None], (count,) + block.shape), axes)
+
+
+def swap(values):
+    return lax.ppermute(values, "zl", [(0, 1), (1, 0)])
+
+
+def swap_core(values):
+    return lax.ppermute(values, "core", [(0, 1), (1, 0)])
 
 
 def halves(values):
@@ -42,24 +50,23 @@
     own_rows, rank = old_query.shape
     replicas = lax.axis_size(EXPERT)
     members = lax.axis_size(DP)
-    plane = lax.axis_size(PLANE)
 
     query_low = old_query.astype(bf16)
     query_blocks = spread(query_low.T, DP, members)
-    partner_rows = lax.ppermute(grad_rows, "zl", [(0, 1), (1, 0)])
-    pair_rows = jnp.concatenate([grad_rows, partner_rows], axis=0)
-    query_blocks, pair_rows = lax.optimization_barrier((query_blocks, pair_rows))
-    full_grad = lax.all_gather(pair_rows, PLANE, axis=0, tiled=True)
-    full_query = query_blocks.transpose(1, 0, 2).reshape(rank, width)
-
     live_slots = lax.iota(jnp.int32, slots) < counts[0]
     slot_scale = jnp.where(live_slots, gate_weight[0], jnp.zeros_like(gate_weight[0]))
     weighted = (hidden_local.astype(f32) * slot_scale[:, None]).astype(bf16)
 
+    pair_rows = jnp.concatenate([grad_rows, swap(grad_rows)], axis=0)
+    full_grad = lax.all_gather(pair_rows, PLANE, axis=0, tiled=True)
+    full_query = query_blocks.transpose(1, 0, 2).reshape(rank, width)
+
     slot_query = product(grad_rows, full_query, 1, 1)
-    slot_pair = spread(jnp.concatenate(halves(slot_query), axis=1), DP, members).reshape(slots, 2 * rank)
-    left_pair = product(weighted, slot_pair, 0, 0)
-    left_part = left_pair[:, :rank] + left_pair[:, rank:] + product(error_local, full_query, 1, 1)
+    slot_high, slot_low = halves(slot_query)
+    slot_wide = jnp.concatenate([slot_high, slot_low, jnp.zeros((own_slots, 2 * rank), bf16)], axis=1)
+    all_slots = spread(slot_wide, DP, members).reshape(slots, 4 * rank)
+    left_pair = product(weighted, all_slots, 0, 0)
+    left_part = left_pair[:, :rank] + left_pair[:, rank : 2 * rank] + product(error_local, full_query, 1, 1)
     left_sum = jnp.sum(spread(left_part, EXPERT, replicas), axis=0) / replicas
 
     sum_high, sum_low = halves(left_sum)
@@ -85,9 +92,14 @@
     vector_pair = jnp.concatenate(halves(own_vectors), axis=1)
     query_pair = product(vector_pair, grad_rows, 0, 0) + product(sum_pair, error_local, 0, 0)
     query_part = query_pair[:rank] + query_pair[rank:]
-    query_part = query_part.reshape(rank, members, own_rows).transpose(1, 0, 2)
-    own_part = jnp.sum(exchange(query_part, DP), axis=0)
-    own_sum = jnp.sum(spread(own_part, EXPERT, replicas), axis=0) / replicas
+    first_core = lax.axis_index("core") == 0
+    upper, lower = query_part[: rank // 2], query_part[rank // 2 :]
+    core_part = jnp.where(first_core, upper, lower) + swap_core(jnp.where(first_core, lower, upper))
+    core_part = core_part.reshape(rank // 2, members, own_rows).transpose(1, 0, 2)
+    incoming = exchange(core_part, DP)
+    own_part = jnp.sum(incoming, axis=0)
+    expert_parts = spread(own_part, EXPERT, replicas)
+    own_sum = jnp.sum(expert_parts.reshape(-1, rank, own_rows), axis=0) / replicas
 
     chol_lower = jnp.linalg.cholesky(gram_matrix)
     inverse = lax.linalg.triangular_solve(
@@ -98,22 +110,31 @@
     )
     new_cols = jnp.dot(inverse, own_sum, precision=exact_mode, preferred_element_type=f32)
     new_rows = new_cols.T
-    col_blocks = spread(jnp.concatenate(halves(new_cols), axis=0), DP, members)
+    cols_high, cols_low = halves(new_cols)
+    half_rank = rank // 2
+    sent_cols = jnp.where(
+        first_core,
+        jnp.concatenate([cols_high[:half_rank], cols_low[:half_rank]], axis=0),
+        jnp.concatenate([cols_high[half_rank:], cols_low[half_rank:]], axis=0),
+    )
+    col_blocks = spread(sent_cols, DP, members)
 
     own_first = lax.axis_index("zl") == 0
-    parts = weighted.reshape(2, plane, own_slots, units)
-    ordered = jnp.where(
-        own_first,
-        jnp.stack([parts[0], parts[1]], axis=1),
-        jnp.stack([parts[1], parts[0]], axis=1),
+    parts = weighted.reshape(2, lax.axis_size(PLANE), own_slots, units)
+    ordered = jnp.stack(
+        [jnp.where(own_first, parts[0], parts[1]), jnp.where(own_first, parts[1], parts[0])], axis=1
     ).reshape(slots, units)
     merged = product(ordered, full_grad, 0, 0) + error_local.astype(f32)
     merged, col_blocks = lax.optimization_barrier((merged, col_blocks))
-    col_pair = col_blocks.transpose(1, 0, 2).reshape(2 * rank, width)
-    basis_high, basis_low = halves(left_basis)
+    core_cols = col_blocks.transpose(1, 0, 2).reshape(rank, width)
+    all_cols = jnp.concatenate([core_cols, swap_core(core_cols)], axis=0)
+    left_half, right_half = left_basis[:, :half_rank], left_basis[:, half_rank:]
+    own_high, own_low = halves(jnp.where(first_core, left_half, right_half))
+    other_high, other_low = halves(jnp.where(first_core, right_half, left_half))
+    nothing = jnp.zeros_like(own_low)
     correction = product(
-        jnp.concatenate([basis_high, basis_high], axis=1), col_pair, 1, 0
-    ) + product(basis_low, col_pair[:rank], 1, 0)
+        jnp.concatenate([own_high, own_high, other_high, other_high], axis=1), all_cols, 1, 0
+    ) + product(jnp.concatenate([own_low, nothing, other_low, nothing], axis=1), all_cols, 1, 0)
     new_error = (merged - correction).astype(bf16)
     return (new_error[None], new_rows)
 

time: 226 us -> 218 us (0.965)
  waiting for transfers between devices: 110 us -> 91.7 us
  starting transfers between devices: 60.7 us -> 74.3 us
  local copies, waits for them, and re-layouts: 12.1 us -> 8.66 us
    all_gather x1, waiting for transfers between devices: 21.5 us -> 0.02 us  [body(): full_grad = lax.all_gather(pair_rows, PLANE, axis=0, tiled=True)]
    ppermute x1 -> x3, starting transfers between devices: 4.96 us -> 15 us  [the longest x2 10.2 us: swap_core(): return lax.ppermute(values, 'core', [(0, 1), (1, 0)])]
    ppermute x1 -> x3, waiting for transfers between devices: 0.01 us -> 4.55 us  [the longest x1 3.25 us: swap(): return lax.ppermute(values, 'zl', [(0, 1), (1, 0)])]
    all_to_all x7, starting transfers between devices: 55.7 us -> 59.3 us  [exchange(): return lax.all_to_all(blocks, axes, split_axis=0, concat_axis=0, tiled=True)]
  transfers between devices with their start and end apart: 9 -> 11, of which waited for: 8 -> 9; matrix products, arithmetic and copies ran while one was open for 14% -> 14% of each run, Pallas kernels for 0% -> 0%
where the time goes in v4:
time: 218 us; the launch traced here: 217 us
  waiting for transfers between devices  91.7 us (42%)
  starting transfers between devices  74.3 us (34%)
  between operations  15 us (7%)
  matrix products  14.1 us (6%)
  other arithmetic  12.9 us (6%)
  local copies, waits for them, and re-layouts  8.66 us (4%)
    all_to_all x7, waiting for transfers between devices, exchange(): return lax.all_to_all(blocks, axes, split_axis=0, concat_axis=0, tiled=True)  87.2 us
    all_to_all x7, starting transfers between devices, exchange(): return lax.all_to_all(blocks, axes, split_axis=0, concat_axis=0, tiled=True)  59.3 us
    dot_general x9, matrix products, product(): lax.dot_general(left_side, right_side, (((left_dim,), (right_dim,)), ((),...  12.8 us
    ppermute x2, starting transfers between devices, swap_core(): return lax.ppermute(values, 'core', [(0, 1), (1, 0)])  10.2 us
    ppermute x1, starting transfers between devices, swap(): return lax.ppermute(values, 'zl', [(0, 1), (1, 0)])  4.83 us
  transfers between devices with their start and end apart: 11, of which 9 were waited for; matrix products, arithmetic and copies ran while one was open for 14% of the time, Pallas kernels for 0%

profile of v4, /device:TPU:1, one launch (start us, length us, event | category | flops | bytes accessed | tf_op | source)
XLA Modules:
  0.0 216.7 jit_solution(13164840186101720743)
XLA Ops:
  7.2 4.8 %collective-permute-start = (bf16[16,6144]{1,0:T(8,128)(2,1)}, bf16[16,6144]{1,0:T(8,128)(2,1)S(1)}, u32[]{:S(2)}, u32[]{:S(2)}) collective-permute-start(bf16[16,6144]{1,0:T(8,128)(2,1)} %bitcast.65), channel_id=1, source_target_pairs={{0,32},{32,0},{1,33},{33,1},{2,34},{34,2},{3,35},{35,3},{4,36},{36... | collective-permute-start | bytes 589832 | tf_op jit(solution)/shard_map/ppermute | solution.py:23
  12.0 3.3 %collective-permute-done = bf16[16,6144]{1,0:T(8,128)(2,1)S(1)} collective-permute-done((bf16[16,6144]{1,0:T(8,128)(2,1)}, bf16[16,6144]{1,0:T(8,128)(2,1)S(1)}, u32[]{:S(2)}, u32[]{:S(2)}) %collective-permute-start) | collective-permute-done | bytes 196640 | tf_op jit(solution)/shard_map/ppermute | solution.py:23
  15.3 1.7 pad_maximum_fusion.1
  17.0 0.7 convert_bitcast_fusion.1
  17.8 0.9 broadcast_in_dim.22
  18.6 12.8 %all-to-all-start = ((bf16[64,32,96]{2,1,0:T(8,128)(2,1)}), bf16[64,32,96]{2,1,0:T(8,128)(2,1)S(1)}, u32[]{:S(2)}, u32[]{:S(2)}) async-start(bf16[64,32,96]{2,1,0:T(8,128)(2,1)} %broadcast_in_dim.22), calls=%async_computation | async-start | bytes 1048576 | tf_op jit(solution)/shard_map/all_to_all | solution.py:15
  31.5 0.1 pad.26.clone
  31.6 14.5 %all-to-all-done = bf16[64,32,96]{2,1,0:T(8,128)(2,1)S(1)} async-done(((bf16[64,32,96]{2,1,0:T(8,128)(2,1)}), bf16[64,32,96]{2,1,0:T(8,128)(2,1)S(1)}, u32[]{:S(2)}, u32[]{:S(2)}) %all-to-all-start) | async-done | bytes 393248 | tf_op jit(solution)/shard_map/all_to_all | solution.py:15
  46.1 0.2 copy.21
  46.3 0.7 reshape.131
  47.1 0.2 reduce-precision_convert_fusion.5
  47.3 0.1 maximum_maximum_fusion
  47.4 0.8 broadcast_in_dim.24
  48.1 8.4 %all-to-all-start.1 = ((bf16[64,16,128]{2,1,0:T(8,128)(2,1)}), bf16[64,16,128]{2,1,0:T(8,128)(2,1)S(1)}, u32[]{:S(2)}, u32[]{:S(2)}) async-start(bf16[64,16,128]{2,1,0:T(8,128)(2,1)} %broadcast_in_dim.24), calls=%async_computation.1 | async-start | bytes 524288 | tf_op jit(solution)/shard_map/all_to_all | solution.py:15
  57.2 10.9 %all-to-all-done.1 = bf16[64,16,128]{2,1,0:T(8,128)(2,1)S(1)} async-done(((bf16[64,16,128]{2,1,0:T(8,128)(2,1)}), bf16[64,16,128]{2,1,0:T(8,128)(2,1)S(1)}, u32[]{:S(2)}, u32[]{:S(2)}) %all-to-all-start.1) | async-done | bytes 262176 | tf_op jit(solution)/shard_map/all_to_all | solution.py:15
  68.1 0.4 fusion.18
  68.6 0.6 fusion.7
  69.2 0.7 broadcast_in_dim.26
  69.9 16.4 %all-to-all-start.2 = ((f32[8,128,32]{1,2,0:T(8,128)}), f32[8,128,32]{1,2,0:T(8,128)S(1)}, u32[]{:S(2)}, u32[]{:S(2)}) async-start(f32[8,128,32]{1,2,0:T(8,128)} %broadcast_in_dim.26), calls=%async_computation.2 | async-start | bytes 262144 | tf_op jit(solution)/shard_map/all_to_all | solution.py:15
  86.3 0.2 fusion.11
  86.5 7.9 %all-to-all-done.2 = f32[8,128,32]{1,2,0:T(8,128)S(1)} async-done(((f32[8,128,32]{1,2,0:T(8,128)}), f32[8,128,32]{1,2,0:T(8,128)S(1)}, u32[]{:S(2)}, u32[]{:S(2)}) %all-to-all-start.2) | async-done | bytes 131104 | tf_op jit(solution)/shard_map/all_to_all | solution.py:15
  94.4 0.1 fusion.52
  94.6 0.1 pad_maximum_fusion.4
  94.7 0.3 fusion.13
  95.0 1.0 pad_maximum_fusion
  96.0 6.0 %all-to-all-start.3 = ((f32[64,16,96]{2,1,0:T(8,128)}), f32[64,16,96]{2,1,0:T(8,128)}, u32[]{:S(2)}, u32[]{:S(2)}) async-start(f32[64,16,96]{2,1,0:T(8,128)} %pad_maximum_fusion), calls=%async_computation.3 | async-start | bytes 1048576 | tf_op jit(solution)/shard_map/all_to_all | solution.py:15
  102.0 0.7 pad_maximum_fusion.2
  102.8 0.4 fusion.3
  103.1 19.9 %all-to-all-done.3 = f32[64,16,96]{2,1,0:T(8,128)} async-done(((f32[64,16,96]{2,1,0:T(8,128)}), f32[64,16,96]{2,1,0:T(8,128)}, u32[]{:S(2)}, u32[]{:S(2)}) %all-to-all-start.3) | async-done | bytes 393248 | tf_op jit(solution)/shard_map/all_to_all | solution.py:15
  123.0 1.1 reduce_sum.37
  124.2 0.1 reduce-precision_convert_fusion.4
  124.3 0.1 copy.30
  124.4 0.5 convolution_add_fusion.2
  124.9 0.1 slice_add_fusion
  125.0 5.6 %collective-permute-start.1 = (f32[16,6144]{1,0:T(8,128)S(1)}, f32[16,6144]{1,0:T(8,128)S(1)}, u32[]{:S(2)}, u32[]{:S(2)}) collective-permute-start(f32[16,6144]{1,0:T(8,128)S(1)} %slice_select_fusion), channel_id=1, source_target_pairs={{0,64},{64,0},{1,65},{65,1},{2,66},{66,2},{3,67},{67,3},{4,68},{68... | collective-permute-start | bytes 1179656 | tf_op jit(solution)/shard_map/ppermute | solution.py:27
  130.6 0.1 pad_maximum_fusion.3
  130.7 0.1 copy.25
  130.7 0.1 fusion.47
  130.8 2.9 %cholesky.17 = f32[32,32]{1,0:T(8,128)S(1)} custom-call(f32[32,32]{1,0:T(8,128)S(1)} %fusion.47), custom_call_target="Cholesky" | custom-call | tf_op jit(solution)/shard_map/jit(cholesky)/cholesky | solution.py:104
  133.9 0.2 reshape.134
  134.1 1.1 copy.32
  135.2 5.3 %all-to-all-start.4 = ((f32[64,16,96]{2,1,0:T(8,128)}), f32[64,16,96]{2,1,0:T(8,128)S(1)}, u32[]{:S(2)}, u32[]{:S(2)}) async-start(f32[64,16,96]{2,1,0:T(8,128)} %bitcast.60), calls=%async_computation.4 | async-start | bytes 1048576 | tf_op jit(solution)/shard_map/all_to_all | solution.py:15
  140.4 0.6 compare_reduce_fusion
  141.1 0.7 fusion.21
  141.7 2.4 %custom-call.6 = f32[1,32,32]{1,2,0:T(8,128)S(1)} custom-call(f32[1,32,32]{2,1,0:T(8,128)S(1)} %fusion.21), custom_call_target="InvertDiagBlocksLowerTriangular" | custom-call | tf_op jit(solution)/shard_map/triangular_solve | solution.py:105
  144.2 0.2 fusion.45
  144.4 0.1 fusion.50
  144.5 19.0 %all-to-all-done.4 = f32[64,16,96]{2,1,0:T(8,128)S(1)} async-done(((f32[64,16,96]{2,1,0:T(8,128)}), f32[64,16,96]{2,1,0:T(8,128)S(1)}, u32[]{:S(2)}, u32[]{:S(2)}) %all-to-all-start.4) | async-done | bytes 393248 | tf_op jit(solution)/shard_map/all_to_all | solution.py:15
  163.5 0.1 reduce_sum.38
  163.6 0.6 broadcast_in_dim.28
  164.3 4.9 %all-to-all-start.5 = ((f32[8,16,96]{2,1,0:T(8,128)}), f32[8,16,96]{2,1,0:T(8,128)S(1)}, u32[]{:S(2)}, u32[]{:S(2)}) async-start(f32[8,16,96]{2,1,0:T(8,128)} %broadcast_in_dim.28), calls=%async_computation.5 | async-start | bytes 131072 | tf_op jit(solution)/shard_map/all_to_all | solution.py:15
  169.2 7.5 %all-to-all-done.5 = f32[8,16,96]{2,1,0:T(8,128)S(1)} async-done(((f32[8,16,96]{2,1,0:T(8,128)}), f32[8,16,96]{2,1,0:T(8,128)S(1)}, u32[]{:S(2)}, u32[]{:S(2)}) %all-to-all-start.5) | async-done | bytes 49184 | tf_op jit(solution)/shard_map/all_to_all | solution.py:15
  176.7 0.8 reduce-precision_convert_fusion
  177.4 0.9 broadcast_in_dim.29
  178.3 5.4 %all-to-all-start.6 = ((bf16[64,32,96]{2,1,0:T(8,128)(2,1)}), bf16[64,32,96]{2,1,0:T(8,128)(2,1)S(1)}, u32[]{:S(2)}, u32[]{:S(2)}) async-start(bf16[64,32,96]{2,1,0:T(8,128)(2,1)} %broadcast_in_dim.29), calls=%async_computation.6 | async-start | bytes 1048576 | tf_op jit(solution)/shard_map/all_to_all | solution.py:15
  183.8 8.1 %convolution_add_fusion.1 = f32[128,6144]{1,0:T(8,128)} fusion(bf16[1024,128]{1,0:T(8,128)(2,1)S(1)} %bitcast.67, bf16[1024,6144]{1,0:T(8,128)(2,1)} %all-gather.2.cloned.1.call-done, bf16[1,128,6144]{2,1,0:T(8,128)(2,1)S(1)} %copy-done), kind=kOutput, calls=%fused_computation.2 | convolution fusion | flops 1612185600 | bytes 17563648 | tf_op jit(solution)/shard_map/dot_general | solution.py:36
  191.9 7.5 %all-to-all-done.6 = bf16[64,32,96]{2,1,0:T(8,128)(2,1)S(1)} async-done(((bf16[64,32,96]{2,1,0:T(8,128)(2,1)}), bf16[64,32,96]{2,1,0:T(8,128)(2,1)S(1)}, u32[]{:S(2)}, u32[]{:S(2)}) %all-to-all-start.6) | async-done | bytes 393248 | tf_op jit(solution)/shard_map/all_to_all | solution.py:15
  199.3 0.2 copy.27
  199.5 0.7 reshape.136
  200.3 4.6 %collective-permute-start.2 = (bf16[32,6144]{1,0:T(8,128)(2,1)S(1)}, bf16[32,6144]{1,0:T(8,128)(2,1)S(1)}, u32[]{:S(2)}, u32[]{:S(2)}) collective-permute-start(bf16[32,6144]{1,0:T(8,128)(2,1)S(1)} %reshape.136), channel_id=1, source_target_pairs={{0,64},{64,0},{1,65},{65,1},{2,66},{66,2},{3,67},{67,3},{4,68},{68... | collective-permute-start | bytes 1179656 | tf_op jit(solution)/shard_map/ppermute | solution.py:27
  204.9 1.3 collective-permute-done.2
  206.2 0.6 fusion.37
  206.8 1.3 copy-done.1
  208.1 1.7 fusion.2
  (33 shorter events, 0.5 us)
Async XLA Ops:
  7.2 176.6 %all-gather.2.cloned.1.call-start = ((), (), s32[]{:S(2)}) async-start(), calls=%async_computation.7 | async-start | bytes 12976128 | tf_op jit(solution)/shard_map/all_gather | solution.py:61
  7.2 8.1 %collective-permute-start = (bf16[16,6144]{1,0:T(8,128)(2,1)}, bf16[16,6144]{1,0:T(8,128)(2,1)S(1)}, u32[]{:S(2)}, u32[]{:S(2)}) collective-permute-start(bf16[16,6144]{1,0:T(8,128)(2,1)} %bitcast.65), channel_id=1, source_target_pairs={{0,32},{32,0},{1,33},{33,1},{2,34},{34,2},{3,35},{35,3},{4,36},{36... | collective-permute-start | bytes 589832 | tf_op jit(solution)/shard_map/ppermute | solution.py:23
  18.6 28.4 %copy-start.2 = (bf16[1,16,6144]{2,1,0:T(8,128)(2,1)S(1)}, bf16[1,16,6144]{2,1,0:T(8,128)(2,1)}, u32[]{:S(2)}) copy-start(bf16[1,16,6144]{2,1,0:T(8,128)(2,1)} %param.7) | copy-start | bytes 589828
  18.6 27.5 %all-to-all-start = ((bf16[64,32,96]{2,1,0:T(8,128)(2,1)}), bf16[64,32,96]{2,1,0:T(8,128)(2,1)S(1)}, u32[]{:S(2)}, u32[]{:S(2)}) async-start(bf16[64,32,96]{2,1,0:T(8,128)(2,1)} %broadcast_in_dim.22), calls=%async_computation | async-start | bytes 1048576 | tf_op jit(solution)/shard_map/all_to_all | solution.py:15
  46.1 11.1 %copy-start.5 = (f32[1,1024]{1,0:T(1,128)S(1)}, f32[1,1024]{1,0:T(1,128)}, u32[]{:S(2)}) copy-start(f32[1,1024]{1,0:T(1,128)} %param.8) | copy-start | bytes 12292
  46.1 22.0 %copy-start.4 = (bf16[1,1024,128]{2,1,0:T(8,128)(2,1)S(1)}, bf16[1,1024,128]{2,1,0:T(8,128)(2,1)}, u32[]{:S(2)}) copy-start(bf16[1,1024,128]{2,1,0:T(8,128)(2,1)} %param.6) | copy-start | bytes 786436
  46.3 22.2 %copy-start = (bf16[1,128,6144]{2,1,0:T(8,128)(2,1)S(1)}, bf16[1,128,6144]{2,1,0:T(8,128)(2,1)}, u32[]{:S(2)}) copy-start(bf16[1,128,6144]{2,1,0:T(8,128)(2,1)} %param.10) | copy-start | bytes 4718596
  48.1 20.0 %all-to-all-start.1 = ((bf16[64,16,128]{2,1,0:T(8,128)(2,1)}), bf16[64,16,128]{2,1,0:T(8,128)(2,1)S(1)}, u32[]{:S(2)}, u32[]{:S(2)}) async-start(bf16[64,16,128]{2,1,0:T(8,128)(2,1)} %broadcast_in_dim.24), calls=%async_computation.1 | async-start | bytes 524288 | tf_op jit(solution)/shard_map/all_to_all | solution.py:15
  69.9 24.5 %all-to-all-start.2 = ((f32[8,128,32]{1,2,0:T(8,128)}), f32[8,128,32]{1,2,0:T(8,128)S(1)}, u32[]{:S(2)}, u32[]{:S(2)}) async-start(f32[8,128,32]{1,2,0:T(8,128)} %broadcast_in_dim.26), calls=%async_computation.2 | async-start | bytes 262144 | tf_op jit(solution)/shard_map/all_to_all | solution.py:15
  96.0 27.1 %all-to-all-start.3 = ((f32[64,16,96]{2,1,0:T(8,128)}), f32[64,16,96]{2,1,0:T(8,128)}, u32[]{:S(2)}, u32[]{:S(2)}) async-start(f32[64,16,96]{2,1,0:T(8,128)} %pad_maximum_fusion), calls=%async_computation.3 | async-start | bytes 1048576 | tf_op jit(solution)/shard_map/all_to_all | solution.py:15
  125.0 8.8 %collective-permute-start.1 = (f32[16,6144]{1,0:T(8,128)S(1)}, f32[16,6144]{1,0:T(8,128)S(1)}, u32[]{:S(2)}, u32[]{:S(2)}) collective-permute-start(f32[16,6144]{1,0:T(8,128)S(1)} %slice_select_fusion), channel_id=1, source_target_pairs={{0,64},{64,0},{1,65},{65,1},{2,66},{66,2},{3,67},{67,3},{4,68},{68... | collective-permute-start | bytes 1179656 | tf_op jit(solution)/shard_map/ppermute | solution.py:27
  135.2 28.4 %all-to-all-start.4 = ((f32[64,16,96]{2,1,0:T(8,128)}), f32[64,16,96]{2,1,0:T(8,128)S(1)}, u32[]{:S(2)}, u32[]{:S(2)}) async-start(f32[64,16,96]{2,1,0:T(8,128)} %bitcast.60), calls=%async_computation.4 | async-start | bytes 1048576 | tf_op jit(solution)/shard_map/all_to_all | solution.py:15
  140.4 43.3 %copy-start.3 = (bf16[32,2,16,128]{3,2,1,0:T(8,128)(2,1)S(1)}, bf16[32,2,16,128]{3,2,1,0:T(8,128)(2,1)}, u32[]{:S(2)}) copy-start(bf16[32,2,16,128]{3,2,1,0:T(8,128)(2,1)} %pad_maximum_fusion.2) | copy-start | bytes 786436
  164.3 12.4 %all-to-all-start.5 = ((f32[8,16,96]{2,1,0:T(8,128)}), f32[8,16,96]{2,1,0:T(8,128)S(1)}, u32[]{:S(2)}, u32[]{:S(2)}) async-start(f32[8,16,96]{2,1,0:T(8,128)} %broadcast_in_dim.28), calls=%async_computation.5 | async-start | bytes 131072 | tf_op jit(solution)/shard_map/all_to_all | solution.py:15
  178.3 21.1 %all-to-all-start.6 = ((bf16[64,32,96]{2,1,0:T(8,128)(2,1)}), bf16[64,32,96]{2,1,0:T(8,128)(2,1)S(1)}, u32[]{:S(2)}, u32[]{:S(2)}) async-start(bf16[64,32,96]{2,1,0:T(8,128)(2,1)} %broadcast_in_dim.29), calls=%async_computation.6 | async-start | bytes 1048576 | tf_op jit(solution)/shard_map/all_to_all | solution.py:15
  200.3 5.9 %collective-permute-start.2 = (bf16[32,6144]{1,0:T(8,128)(2,1)S(1)}, bf16[32,6144]{1,0:T(8,128)(2,1)S(1)}, u32[]{:S(2)}, u32[]{:S(2)}) collective-permute-start(bf16[32,6144]{1,0:T(8,128)(2,1)S(1)} %reshape.136), channel_id=1, source_target_pairs={{0,64},{64,0},{1,65},{65,1},{2,66},{66,2},{3,67},{67,3},{4,68},{68... | collective-permute-start | bytes 1179656 | tf_op jit(solution)/shard_map/ppermute | solution.py:27
  206.2 1.9 copy-start.1
Sparse Core Ops, SparseCore 0:
  17.2 155.3 all-gather.1

commit v5 on v4

--- a/solution.py
+++ b/solution.py
@@ -25,6 +25,16 @@
 
 def swap_core(values):
     return lax.ppermute(values, "core", [(0, 1), (1, 0)])
+
+
+def fold(blocks):
+    middle = blocks.shape[1] // 2
+    return jnp.concatenate([blocks[:, :middle], blocks[:, middle:]], axis=2)
+
+
+def unfold(values):
+    middle = values.shape[1] // 2
+    return jnp.concatenate([values[:, :middle], values[:, middle:]], axis=0)
 
 
 def halves(values):
@@ -58,6 +68,7 @@
     weighted = (hidden_local.astype(f32) * slot_scale[:, None]).astype(bf16)
 
     pair_rows = jnp.concatenate([grad_rows, swap(grad_rows)], axis=0)
+    query_blocks, pair_rows = lax.optimization_barrier((query_blocks, pair_rows))
     full_grad = lax.all_gather(pair_rows, PLANE, axis=0, tiled=True)
     full_query = query_blocks.transpose(1, 0, 2).reshape(rank, width)
 
@@ -76,23 +87,28 @@
     gram_part = lax.dot_general(
         left_sum, left_sum, (((0,), (0,)), ((), ())), precision=exact_mode, preferred_element_type=f32
     )
-    gram_wide = jnp.concatenate([gram_part[:own_slots], gram_part[own_slots:]], axis=1)
+    first_core = lax.axis_index("core") == 0
+    half_rank = rank // 2
+    gram_half = jnp.where(first_core, gram_part[:half_rank], gram_part[half_rank:])
     outgoing = jnp.concatenate(
         [
-            slot_parts.reshape(members, own_slots, rank),
-            jnp.broadcast_to(gram_wide[None], (members,) + gram_wide.shape),
+            fold(slot_parts.reshape(members, own_slots, rank)),
+            jnp.broadcast_to(fold(gram_half[None]), (members, half_rank // 2, 2 * rank)),
         ],
         axis=2,
     )
     summed = jnp.sum(exchange(outgoing, DP), axis=0)
-    own_vectors = summed[:, :rank]
-    gram_matrix = jnp.concatenate([summed[:, rank : 2 * rank], summed[:, 2 * rank :]], axis=0)
+    own_vectors = unfold(summed[:, : 2 * rank])
+    gram_half = unfold(summed[:, 2 * rank :])
+    other_half = swap_core(gram_half)
+    gram_matrix = jnp.concatenate(
+        [jnp.where(first_core, gram_half, other_half), jnp.where(first_core, other_half, gram_half)], axis=0
+    )
 
     sum_pair = jnp.concatenate([sum_high, sum_low], axis=1)
     vector_pair = jnp.concatenate(halves(own_vectors), axis=1)
     query_pair = product(vector_pair, grad_rows, 0, 0) + product(sum_pair, error_local, 0, 0)
     query_part = query_pair[:rank] + query_pair[rank:]
-    first_core = lax.axis_index("core") == 0
     upper, lower = query_part[: rank // 2], query_part[rank // 2 :]
     core_part = jnp.where(first_core, upper, lower) + swap_core(jnp.where(first_core, lower, upper))
     core_part = core_part.reshape(rank // 2, members, own_rows).transpose(1, 0, 2)
@@ -111,7 +127,6 @@
     new_cols = jnp.dot(inverse, own_sum, precision=exact_mode, preferred_element_type=f32)
     new_rows = new_cols.T
     cols_high, cols_low = halves(new_cols)
-    half_rank = rank // 2
     sent_cols = jnp.where(
         first_core,
         jnp.concatenate([cols_high[:half_rank], cols_low[:half_rank]], axis=0),

time: 218 us -> 212 us (0.972)
  starting transfers between devices: 74.3 us -> 65.9 us
  waiting for transfers between devices: 91.7 us -> 95 us
    all_gather x1, waiting for transfers between devices: 0.02 us -> 25.3 us  [body(): full_grad = lax.all_gather(pair_rows, PLANE, axis=0, tiled=True)]
    all_to_all x7, waiting for transfers between devices: 87.2 us -> 68.4 us  [exchange(): return lax.all_to_all(blocks, axes, split_axis=0, concat_axis=0, tiled=True)]
    all_to_all x7, starting transfers between devices: 59.3 us -> 51.2 us  [exchange(): return lax.all_to_all(blocks, axes, split_axis=0, concat_axis=0, tiled=True)]
    ppermute x1, waiting for transfers between devices: 3.25 us -> 0.01 us  [swap(): return lax.ppermute(values, 'zl', [(0, 1), (1, 0)])]
    ppermute x2 -> x3, starting transfers between devices: 10.2 us -> 9.7 us  [swap_core(): return lax.ppermute(values, 'core', [(0, 1), (1, 0)])]
  transfers between devices with their start and end apart: 11 -> 12, of which waited for: 9 -> 8; matrix products, arithmetic and copies ran while one was open for 14% -> 14% of each run, Pallas kernels for 0% -> 0%
where the time goes in v5:
time: 212 us; the launch traced here: 211 us
  waiting for transfers between devices  95 us (45%)
  starting transfers between devices  65.9 us (31%)
  between operations  15 us (7%)
  matrix products  14.1 us (7%)
  other arithmetic  12 us (6%)
  local copies, waits for them, and re-layouts  8.96 us (4%)
    all_to_all x7, waiting for transfers between devices, exchange(): return lax.all_to_all(blocks, axes, split_axis=0, concat_axis=0, tiled=True)  68.4 us
    all_to_all x7, starting transfers between devices, exchange(): return lax.all_to_all(blocks, axes, split_axis=0, concat_axis=0, tiled=True)  51.2 us
    all_gather x1, waiting for transfers between devices, body(): full_grad = lax.all_gather(pair_rows, PLANE, axis=0, tiled=True)  25.3 us
    dot_general x9, matrix products, product(): lax.dot_general(left_side, right_side, (((left_dim,), (right_dim,)), ((),...  12.8 us
    ppermute x3, starting transfers between devices, swap_core(): return lax.ppermute(values, 'core', [(0, 1), (1, 0)])  9.7 us
    ppermute x1, starting transfers between devices, swap(): return lax.ppermute(values, 'zl', [(0, 1), (1, 0)])  4.96 us
  transfers between devices with their start and end apart: 12, of which 8 were waited for; matrix products, arithmetic and copies ran while one was open for 14% of the time, Pallas kernels for 0%

profile of v5, /device:TPU:1, one launch (start us, length us, event | category | flops | bytes accessed | tf_op | source)
XLA Modules:
  0.0 210.9 jit_solution(12775766779230714792)
XLA Ops:
  7.2 5.0 %collective-permute-start = (bf16[16,6144]{1,0:T(8,128)(2,1)}, bf16[16,6144]{1,0:T(8,128)(2,1)S(1)}, u32[]{:S(2)}, u32[]{:S(2)}) collective-permute-start(bf16[16,6144]{1,0:T(8,128)(2,1)} %bitcast.77), channel_id=1, source_target_pairs={{0,32},{32,0},{1,33},{33,1},{2,34},{34,2},{3,35},{35,3},{4,36},{36... | collective-permute-start | bytes 589832 | tf_op jit(solution)/shard_map/ppermute | solution.py:23
  12.1 0.7 convert_bitcast_fusion.1
  12.9 0.9 broadcast_in_dim.27
  13.7 10.3 %all-to-all-start = ((bf16[64,32,96]{2,1,0:T(8,128)(2,1)}), bf16[64,32,96]{2,1,0:T(8,128)(2,1)S(1)}, u32[]{:S(2)}, u32[]{:S(2)}) async-start(bf16[64,32,96]{2,1,0:T(8,128)(2,1)} %broadcast_in_dim.27), calls=%async_computation | async-start | bytes 1048576 | tf_op jit(solution)/shard_map/all_to_all | solution.py:15
  24.1 0.8 pad_maximum_fusion
  24.9 14.8 %all-to-all-done = bf16[64,32,96]{2,1,0:T(8,128)(2,1)S(1)} async-done(((bf16[64,32,96]{2,1,0:T(8,128)(2,1)}), bf16[64,32,96]{2,1,0:T(8,128)(2,1)S(1)}, u32[]{:S(2)}, u32[]{:S(2)}) %all-to-all-start) | async-done | bytes 393248 | tf_op jit(solution)/shard_map/all_to_all | solution.py:15
  39.9 0.2 copy.32
  40.1 0.7 reshape.130
  40.8 0.2 reduce-precision_convert_fusion.5
  41.0 0.1 maximum_maximum_fusion
  41.1 0.8 broadcast_in_dim.29
  41.9 6.8 %all-to-all-start.1 = ((bf16[64,16,128]{2,1,0:T(8,128)(2,1)}), bf16[64,16,128]{2,1,0:T(8,128)(2,1)S(1)}, u32[]{:S(2)}, u32[]{:S(2)}) async-start(bf16[64,16,128]{2,1,0:T(8,128)(2,1)} %broadcast_in_dim.29), calls=%async_computation.1 | async-start | bytes 524288 | tf_op jit(solution)/shard_map/all_to_all | solution.py:15
  49.4 10.0 %all-to-all-done.1 = bf16[64,16,128]{2,1,0:T(8,128)(2,1)S(1)} async-done(((bf16[64,16,128]{2,1,0:T(8,128)(2,1)}), bf16[64,16,128]{2,1,0:T(8,128)(2,1)S(1)}, u32[]{:S(2)}, u32[]{:S(2)}) %all-to-all-start.1) | async-done | bytes 262176 | tf_op jit(solution)/shard_map/all_to_all | solution.py:15
  59.4 0.4 fusion.21
  59.8 0.6 fusion.10
  60.5 0.7 broadcast_in_dim.30
  61.2 13.1 %all-to-all-start.2 = ((f32[8,128,32]{1,2,0:T(8,128)}), f32[8,128,32]{1,2,0:T(8,128)S(1)}, u32[]{:S(2)}, u32[]{:S(2)}) async-start(f32[8,128,32]{1,2,0:T(8,128)} %broadcast_in_dim.30), calls=%async_computation.2 | async-start | bytes 262144 | tf_op jit(solution)/shard_map/all_to_all | solution.py:15
  74.2 0.2 fusion.14
  74.4 7.8 %all-to-all-done.2 = f32[8,128,32]{1,2,0:T(8,128)S(1)} async-done(((f32[8,128,32]{1,2,0:T(8,128)}), f32[8,128,32]{1,2,0:T(8,128)S(1)}, u32[]{:S(2)}, u32[]{:S(2)}) %all-to-all-start.2) | async-done | bytes 131104 | tf_op jit(solution)/shard_map/all_to_all | solution.py:15
  82.3 0.1 fusion.56
  82.4 0.1 fusion.27
  82.7 0.1 maximum_bitcast_fusion
  82.8 0.3 fusion.16
  83.1 0.9 pad_maximum_fusion.2
  84.0 5.8 %all-to-all-start.3 = ((f32[64,8,128]{2,1,0:T(8,128)}), f32[64,8,128]{2,1,0:T(8,128)}, u32[]{:S(2)}, u32[]{:S(2)}) async-start(f32[64,8,128]{2,1,0:T(8,128)} %pad_maximum_fusion.2), calls=%async_computation.3 | async-start | bytes 524288 | tf_op jit(solution)/shard_map/all_to_all | solution.py:15
  89.9 0.7 pad_maximum_fusion.1
  90.6 0.4 fusion.3
  91.0 9.4 %all-to-all-done.3 = f32[64,8,128]{2,1,0:T(8,128)} async-done(((f32[64,8,128]{2,1,0:T(8,128)}), f32[64,8,128]{2,1,0:T(8,128)}, u32[]{:S(2)}, u32[]{:S(2)}) %all-to-all-start.3) | async-done | bytes 262176 | tf_op jit(solution)/shard_map/all_to_all | solution.py:15
  100.4 1.0 reduce_sum.37
  101.5 0.1 copy.45
  101.7 0.1 pad_maximum_fusion.3
  101.7 5.4 %collective-permute-start.1 = (f32[16,32]{0,1:T(8,128)S(1)}, f32[16,32]{0,1:T(8,128)S(1)}, u32[]{:S(2)}, u32[]{:S(2)}) collective-permute-start(f32[16,32]{0,1:T(8,128)S(1)} %pad_maximum_fusion.3), channel_id=1, source_target_pairs={{0,64},{64,0},{1,65},{65,1},{2,66},{66,2},{3,67},{67,3},{4,68},{68... | collective-permute-start | bytes 6152 | tf_op jit(solution)/shard_map/ppermute | solution.py:27
  107.1 0.5 convolution_add_fusion.2
  107.6 0.1 slice_add_fusion
  107.7 1.9 collective-permute-start.2
  109.7 0.1 broadcast_select_fusion.3
  109.8 0.1 pad_maximum_fusion.4
  109.9 0.1 fusion.51
  110.0 2.9 %cholesky.17 = f32[32,32]{1,0:T(8,128)S(1)} custom-call(f32[32,32]{1,0:T(8,128)S(1)} %fusion.51), custom_call_target="Cholesky" | custom-call | tf_op jit(solution)/shard_map/jit(cholesky)/cholesky | solution.py:120
  113.0 0.2 reshape.133
  113.2 1.1 copy.48
  114.3 4.6 %all-to-all-start.4 = ((f32[64,16,96]{2,1,0:T(8,128)}), f32[64,16,96]{2,1,0:T(8,128)S(1)}, u32[]{:S(2)}, u32[]{:S(2)}) async-start(f32[64,16,96]{2,1,0:T(8,128)} %bitcast.72), calls=%async_computation.4 | async-start | bytes 1048576 | tf_op jit(solution)/shard_map/all_to_all | solution.py:15
  119.0 0.6 compare_reduce_fusion
  119.6 0.7 fusion.24
  120.3 2.4 %custom-call.6 = f32[1,32,32]{1,2,0:T(8,128)S(1)} custom-call(f32[1,32,32]{2,1,0:T(8,128)S(1)} %fusion.24), custom_call_target="InvertDiagBlocksLowerTriangular" | custom-call | tf_op jit(solution)/shard_map/triangular_solve | solution.py:121
  122.7 0.2 fusion.49
  122.9 0.1 fusion.54
  123.1 18.8 %all-to-all-done.4 = f32[64,16,96]{2,1,0:T(8,128)S(1)} async-done(((f32[64,16,96]{2,1,0:T(8,128)}), f32[64,16,96]{2,1,0:T(8,128)S(1)}, u32[]{:S(2)}, u32[]{:S(2)}) %all-to-all-start.4) | async-done | bytes 393248 | tf_op jit(solution)/shard_map/all_to_all | solution.py:15
  141.9 0.1 reduce_sum.38
  141.9 0.6 broadcast_in_dim.63
  142.6 5.0 %all-to-all-start.5 = ((f32[8,16,96]{2,1,0:T(8,128)}), f32[8,16,96]{2,1,0:T(8,128)S(1)}, u32[]{:S(2)}, u32[]{:S(2)}) async-start(f32[8,16,96]{2,1,0:T(8,128)} %broadcast_in_dim.63), calls=%async_computation.5 | async-start | bytes 131072 | tf_op jit(solution)/shard_map/all_to_all | solution.py:15
  147.6 7.5 %all-to-all-done.5 = f32[8,16,96]{2,1,0:T(8,128)S(1)} async-done(((f32[8,16,96]{2,1,0:T(8,128)}), f32[8,16,96]{2,1,0:T(8,128)S(1)}, u32[]{:S(2)}, u32[]{:S(2)}) %all-to-all-start.5) | async-done | bytes 49184 | tf_op jit(solution)/shard_map/all_to_all | solution.py:15
  155.1 0.8 reduce-precision_convert_fusion
  155.8 0.9 broadcast_in_dim.64
  156.7 5.6 %all-to-all-start.6 = ((bf16[64,32,96]{2,1,0:T(8,128)(2,1)}), bf16[64,32,96]{2,1,0:T(8,128)(2,1)S(1)}, u32[]{:S(2)}, u32[]{:S(2)}) async-start(bf16[64,32,96]{2,1,0:T(8,128)(2,1)} %broadcast_in_dim.64), calls=%async_computation.6 | async-start | bytes 1048576 | tf_op jit(solution)/shard_map/all_to_all | solution.py:15
  162.3 25.3 %all-gather.2.cloned.1.call-done = bf16[1024,6144]{1,0:T(8,128)(2,1)} async-done(((bf16[32,6144]{1,0:T(8,128)(2,1)}), bf16[1024,6144]{1,0:T(8,128)(2,1)}) %all-gather.2.cloned.1.call-update) | async-done | bytes 12582928 | tf_op jit(solution)/shard_map/all_gather | solution.py:72
  187.6 8.1 %convolution_add_fusion.1 = f32[128,6144]{1,0:T(8,128)} fusion(bf16[1024,128]{1,0:T(8,128)(2,1)S(1)} %bitcast.79, bf16[1024,6144]{1,0:T(8,128)(2,1)} %all-gather.2.cloned.1.call-done, bf16[1,128,6144]{2,1,0:T(8,128)(2,1)S(1)} %copy-done), kind=kOutput, calls=%fused_computation.2 | convolution fusion | flops 1612185600 | bytes 17563648 | tf_op jit(solution)/shard_map/dot_general | solution.py:46
  195.8 0.2 copy.42
  196.0 0.7 reshape.135
  196.7 2.4 %collective-permute-start.3 = (bf16[32,6144]{1,0:T(8,128)(2,1)S(1)}, bf16[32,6144]{1,0:T(8,128)(2,1)S(1)}, u32[]{:S(2)}, u32[]{:S(2)}) collective-permute-start(bf16[32,6144]{1,0:T(8,128)(2,1)S(1)} %reshape.135), channel_id=1, source_target_pairs={{0,64},{64,0},{1,65},{65,1},{2,66},{66,2},{3,67},{67,3},{4,68},{68... | collective-permute-start | bytes 1179656 | tf_op jit(solution)/shard_map/ppermute | solution.py:27
  199.1 1.3 collective-permute-done.3
  200.5 0.6 fusion.41
  201.1 1.3 copy-done.1
  202.4 1.7 fusion.2
  (42 shorter events, 0.9 us)
Async XLA Ops:
  7.2 16.9 %copy-start.2 = (bf16[1,16,6144]{2,1,0:T(8,128)(2,1)S(1)}, bf16[1,16,6144]{2,1,0:T(8,128)(2,1)}, u32[]{:S(2)}) copy-start(bf16[1,16,6144]{2,1,0:T(8,128)(2,1)} %param.7) | copy-start | bytes 589828
  7.2 16.9 %collective-permute-start = (bf16[16,6144]{1,0:T(8,128)(2,1)}, bf16[16,6144]{1,0:T(8,128)(2,1)S(1)}, u32[]{:S(2)}, u32[]{:S(2)}) collective-permute-start(bf16[16,6144]{1,0:T(8,128)(2,1)} %bitcast.77), channel_id=1, source_target_pairs={{0,32},{32,0},{1,33},{33,1},{2,34},{34,2},{3,35},{35,3},{4,36},{36... | collective-permute-start | bytes 589832 | tf_op jit(solution)/shard_map/ppermute | solution.py:23
  13.7 26.0 %all-to-all-start = ((bf16[64,32,96]{2,1,0:T(8,128)(2,1)}), bf16[64,32,96]{2,1,0:T(8,128)(2,1)S(1)}, u32[]{:S(2)}, u32[]{:S(2)}) async-start(bf16[64,32,96]{2,1,0:T(8,128)(2,1)} %broadcast_in_dim.27), calls=%async_computation | async-start | bytes 1048576 | tf_op jit(solution)/shard_map/all_to_all | solution.py:15
  24.0 163.6 %all-gather.2.cloned.1.call-start = ((), (), s32[]{:S(2)}) async-start(), calls=%async_computation.7 | async-start | bytes 12976128 | tf_op jit(solution)/shard_map/all_gather | solution.py:72
  39.9 9.5 %copy-start.5 = (f32[1,1024]{1,0:T(1,128)S(1)}, f32[1,1024]{1,0:T(1,128)}, u32[]{:S(2)}) copy-start(f32[1,1024]{1,0:T(1,128)} %param.8) | copy-start | bytes 12292
  39.9 19.5 %copy-start.4 = (bf16[1,1024,128]{2,1,0:T(8,128)(2,1)S(1)}, bf16[1,1024,128]{2,1,0:T(8,128)(2,1)}, u32[]{:S(2)}) copy-start(bf16[1,1024,128]{2,1,0:T(8,128)(2,1)} %param.6) | copy-start | bytes 786436
  40.1 19.8 %copy-start = (bf16[1,128,6144]{2,1,0:T(8,128)(2,1)S(1)}, bf16[1,128,6144]{2,1,0:T(8,128)(2,1)}, u32[]{:S(2)}) copy-start(bf16[1,128,6144]{2,1,0:T(8,128)(2,1)} %param.10) | copy-start | bytes 4718596
  41.9 17.5 %all-to-all-start.1 = ((bf16[64,16,128]{2,1,0:T(8,128)(2,1)}), bf16[64,16,128]{2,1,0:T(8,128)(2,1)S(1)}, u32[]{:S(2)}, u32[]{:S(2)}) async-start(bf16[64,16,128]{2,1,0:T(8,128)(2,1)} %broadcast_in_dim.29), calls=%async_computation.1 | async-start | bytes 524288 | tf_op jit(solution)/shard_map/all_to_all | solution.py:15
  61.2 21.1 %all-to-all-start.2 = ((f32[8,128,32]{1,2,0:T(8,128)}), f32[8,128,32]{1,2,0:T(8,128)S(1)}, u32[]{:S(2)}, u32[]{:S(2)}) async-start(f32[8,128,32]{1,2,0:T(8,128)} %broadcast_in_dim.30), calls=%async_computation.2 | async-start | bytes 262144 | tf_op jit(solution)/shard_map/all_to_all | solution.py:15
  84.0 16.3 %all-to-all-start.3 = ((f32[64,8,128]{2,1,0:T(8,128)}), f32[64,8,128]{2,1,0:T(8,128)}, u32[]{:S(2)}, u32[]{:S(2)}) async-start(f32[64,8,128]{2,1,0:T(8,128)} %pad_maximum_fusion.2), calls=%async_computation.3 | async-start | bytes 524288 | tf_op jit(solution)/shard_map/all_to_all | solution.py:15
  101.7 7.9 %collective-permute-start.1 = (f32[16,32]{0,1:T(8,128)S(1)}, f32[16,32]{0,1:T(8,128)S(1)}, u32[]{:S(2)}, u32[]{:S(2)}) collective-permute-start(f32[16,32]{0,1:T(8,128)S(1)} %pad_maximum_fusion.3), channel_id=1, source_target_pairs={{0,64},{64,0},{1,65},{65,1},{2,66},{66,2},{3,67},{67,3},{4,68},{68... | collective-permute-start | bytes 6152 | tf_op jit(solution)/shard_map/ppermute | solution.py:27
  107.7 5.2 %collective-permute-start.2 = (f32[16,6144]{1,0:T(8,128)S(1)}, f32[16,6144]{1,0:T(8,128)S(1)}, u32[]{:S(2)}, u32[]{:S(2)}) collective-permute-start(f32[16,6144]{1,0:T(8,128)S(1)} %slice_select_fusion), channel_id=1, source_target_pairs={{0,64},{64,0},{1,65},{65,1},{2,66},{66,2},{3,67},{67,3},{4,68},{68... | collective-permute-start | bytes 1179656 | tf_op jit(solution)/shard_map/ppermute | solution.py:27
  114.3 27.5 %all-to-all-start.4 = ((f32[64,16,96]{2,1,0:T(8,128)}), f32[64,16,96]{2,1,0:T(8,128)S(1)}, u32[]{:S(2)}, u32[]{:S(2)}) async-start(f32[64,16,96]{2,1,0:T(8,128)} %bitcast.72), calls=%async_computation.4 | async-start | bytes 1048576 | tf_op jit(solution)/shard_map/all_to_all | solution.py:15
  119.0 68.7 %copy-start.3 = (bf16[32,2,16,128]{3,2,1,0:T(8,128)(2,1)S(1)}, bf16[32,2,16,128]{3,2,1,0:T(8,128)(2,1)}, u32[]{:S(2)}) copy-start(bf16[32,2,16,128]{3,2,1,0:T(8,128)(2,1)} %pad_maximum_fusion.1) | copy-start | bytes 786436
  142.6 12.5 %all-to-all-start.5 = ((f32[8,16,96]{2,1,0:T(8,128)}), f32[8,16,96]{2,1,0:T(8,128)S(1)}, u32[]{:S(2)}, u32[]{:S(2)}) async-start(f32[8,16,96]{2,1,0:T(8,128)} %broadcast_in_dim.63), calls=%async_computation.5 | async-start | bytes 131072 | tf_op jit(solution)/shard_map/all_to_all | solution.py:15
  156.7 39.1 %all-to-all-start.6 = ((bf16[64,32,96]{2,1,0:T(8,128)(2,1)}), bf16[64,32,96]{2,1,0:T(8,128)(2,1)S(1)}, u32[]{:S(2)}, u32[]{:S(2)}) async-start(bf16[64,32,96]{2,1,0:T(8,128)(2,1)} %broadcast_in_dim.64), calls=%async_computation.6 | async-start | bytes 1048576 | tf_op jit(solution)/shard_map/all_to_all | solution.py:15
  196.7 3.7 %collective-permute-start.3 = (bf16[32,6144]{1,0:T(8,128)(2,1)S(1)}, bf16[32,6144]{1,0:T(8,128)(2,1)S(1)}, u32[]{:S(2)}, u32[]{:S(2)}) collective-permute-start(bf16[32,6144]{1,0:T(8,128)(2,1)S(1)} %reshape.135), channel_id=1, source_target_pairs={{0,64},{64,0},{1,65},{65,1},{2,66},{66,2},{3,67},{67,3},{4,68},{68... | collective-permute-start | bytes 1179656 | tf_op jit(solution)/shard_map/ppermute | solution.py:27
  200.5 1.9 copy-start.1
Sparse Core Ops, SparseCore 0:
  39.9 147.6 all-gather.1

commit v6 on v5

--- a/solution.py
+++ b/solution.py
@@ -68,7 +68,6 @@
     weighted = (hidden_local.astype(f32) * slot_scale[:, None]).astype(bf16)
 
     pair_rows = jnp.concatenate([grad_rows, swap(grad_rows)], axis=0)
-    query_blocks, pair_rows = lax.optimization_barrier((query_blocks, pair_rows))
     full_grad = lax.all_gather(pair_rows, PLANE, axis=0, tiled=True)
     full_query = query_blocks.transpose(1, 0, 2).reshape(rank, width)
 

time: 212 us -> 212 us (level)
  waiting for transfers between devices: 95 us -> 82.7 us
  starting transfers between devices: 65.9 us -> 77.5 us
    all_gather x1, waiting for transfers between devices: 25.3 us -> 0.02 us  [body(): full_grad = lax.all_gather(pair_rows, PLANE, axis=0, tiled=True)]
    all_to_all x7, waiting for transfers between devices: 68.4 us -> 78.1 us  [exchange(): return lax.all_to_all(blocks, axes, split_axis=0, concat_axis=0, tiled=True)]
    all_to_all x7, starting transfers between devices: 51.2 us -> 60.1 us  [exchange(): return lax.all_to_all(blocks, axes, split_axis=0, concat_axis=0, tiled=True)]
    ppermute x1, waiting for transfers between devices: 0.01 us -> 3.25 us  [swap(): return lax.ppermute(values, 'zl', [(0, 1), (1, 0)])]
    ppermute x3, starting transfers between devices: 9.7 us -> 12.6 us  [swap_core(): return lax.ppermute(values, 'core', [(0, 1), (1, 0)])]
  transfers between devices with their start and end apart: 12 -> 12, of which waited for: 8 -> 9; matrix products, arithmetic and copies ran while one was open for 14% -> 14% of each run, Pallas kernels for 0% -> 0%
where the time goes in v6:
time: 212 us; the launch traced here: 211 us
  waiting for transfers between devices  82.7 us (39%)
  starting transfers between devices  77.5 us (37%)
  between operations  15 us (7%)
  matrix products  14.1 us (7%)
  other arithmetic  12.9 us (6%)
  local copies, waits for them, and re-layouts  8.96 us (4%)
    all_to_all x7, waiting for transfers between devices, exchange(): return lax.all_to_all(blocks, axes, split_axis=0, concat_axis=0, tiled=True)  78.1 us
    all_to_all x7, starting transfers between devices, exchange(): return lax.all_to_all(blocks, axes, split_axis=0, concat_axis=0, tiled=True)  60.1 us
    dot_general x9, matrix products, product(): lax.dot_general(left_side, right_side, (((left_dim,), (right_dim,)), ((),...  12.8 us
    ppermute x3, starting transfers between devices, swap_core(): return lax.ppermute(values, 'core', [(0, 1), (1, 0)])  12.6 us
    ppermute x1, starting transfers between devices, swap(): return lax.ppermute(values, 'zl', [(0, 1), (1, 0)])  4.83 us
  transfers between devices with their start and end apart: 12, of which 9 were waited for; matrix products, arithmetic and copies ran while one was open for 14% of the time, Pallas kernels for 0%

profile of v6, /device:TPU:1, one launch (start us, length us, event | category | flops | bytes accessed | tf_op | source)
XLA Modules:
  0.0 211.1 jit_solution(11156084446194035533)
XLA Ops:
  7.2 4.8 %collective-permute-start = (bf16[16,6144]{1,0:T(8,128)(2,1)}, bf16[16,6144]{1,0:T(8,128)(2,1)S(1)}, u32[]{:S(2)}, u32[]{:S(2)}) collective-permute-start(bf16[16,6144]{1,0:T(8,128)(2,1)} %bitcast.69), channel_id=1, source_target_pairs={{0,32},{32,0},{1,33},{33,1},{2,34},{34,2},{3,35},{35,3},{4,36},{36... | collective-permute-start | bytes 589832 | tf_op jit(solution)/shard_map/ppermute | solution.py:23
  12.0 3.3 %collective-permute-done = bf16[16,6144]{1,0:T(8,128)(2,1)S(1)} collective-permute-done((bf16[16,6144]{1,0:T(8,128)(2,1)}, bf16[16,6144]{1,0:T(8,128)(2,1)S(1)}, u32[]{:S(2)}, u32[]{:S(2)}) %collective-permute-start) | collective-permute-done | bytes 196640 | tf_op jit(solution)/shard_map/ppermute | solution.py:23
  15.3 1.7 pad_maximum_fusion
  17.1 0.7 convert_bitcast_fusion.1
  17.8 0.9 broadcast_in_dim.27
  18.6 12.8 %all-to-all-start = ((bf16[64,32,96]{2,1,0:T(8,128)(2,1)}), bf16[64,32,96]{2,1,0:T(8,128)(2,1)S(1)}, u32[]{:S(2)}, u32[]{:S(2)}) async-start(bf16[64,32,96]{2,1,0:T(8,128)(2,1)} %broadcast_in_dim.27), calls=%async_computation | async-start | bytes 1048576 | tf_op jit(solution)/shard_map/all_to_all | solution.py:15
  31.6 14.5 %all-to-all-done = bf16[64,32,96]{2,1,0:T(8,128)(2,1)S(1)} async-done(((bf16[64,32,96]{2,1,0:T(8,128)(2,1)}), bf16[64,32,96]{2,1,0:T(8,128)(2,1)S(1)}, u32[]{:S(2)}, u32[]{:S(2)}) %all-to-all-start) | async-done | bytes 393248 | tf_op jit(solution)/shard_map/all_to_all | solution.py:15
  46.1 0.2 copy.32
  46.3 0.7 reshape.130
  47.1 0.2 reduce-precision_convert_fusion.5
  47.3 0.1 maximum_maximum_fusion
  47.4 0.8 broadcast_in_dim.29
  48.1 8.4 %all-to-all-start.1 = ((bf16[64,16,128]{2,1,0:T(8,128)(2,1)}), bf16[64,16,128]{2,1,0:T(8,128)(2,1)S(1)}, u32[]{:S(2)}, u32[]{:S(2)}) async-start(bf16[64,16,128]{2,1,0:T(8,128)(2,1)} %broadcast_in_dim.29), calls=%async_computation.1 | async-start | bytes 524288 | tf_op jit(solution)/shard_map/all_to_all | solution.py:15
  57.2 10.9 %all-to-all-done.1 = bf16[64,16,128]{2,1,0:T(8,128)(2,1)S(1)} async-done(((bf16[64,16,128]{2,1,0:T(8,128)(2,1)}), bf16[64,16,128]{2,1,0:T(8,128)(2,1)S(1)}, u32[]{:S(2)}, u32[]{:S(2)}) %all-to-all-start.1) | async-done | bytes 262176 | tf_op jit(solution)/shard_map/all_to_all | solution.py:15
  68.1 0.4 fusion.18
  68.6 0.6 fusion.7
  69.2 0.7 broadcast_in_dim.30
  69.9 16.4 %all-to-all-start.2 = ((f32[8,128,32]{1,2,0:T(8,128)}), f32[8,128,32]{1,2,0:T(8,128)S(1)}, u32[]{:S(2)}, u32[]{:S(2)}) async-start(f32[8,128,32]{1,2,0:T(8,128)} %broadcast_in_dim.30), calls=%async_computation.2 | async-start | bytes 262144 | tf_op jit(solution)/shard_map/all_to_all | solution.py:15
  86.3 0.2 fusion.11
  86.5 7.9 %all-to-all-done.2 = f32[8,128,32]{1,2,0:T(8,128)S(1)} async-done(((f32[8,128,32]{1,2,0:T(8,128)}), f32[8,128,32]{1,2,0:T(8,128)S(1)}, u32[]{:S(2)}, u32[]{:S(2)}) %all-to-all-start.2) | async-done | bytes 131104 | tf_op jit(solution)/shard_map/all_to_all | solution.py:15
  94.4 0.1 fusion.53
  94.9 0.1 maximum_bitcast_fusion
  94.9 0.3 fusion.13
  95.3 0.9 pad_maximum_fusion.2
  96.2 6.0 %all-to-all-start.3 = ((f32[64,8,128]{2,1,0:T(8,128)}), f32[64,8,128]{2,1,0:T(8,128)}, u32[]{:S(2)}, u32[]{:S(2)}) async-start(f32[64,8,128]{2,1,0:T(8,128)} %pad_maximum_fusion.2), calls=%async_computation.3 | async-start | bytes 524288 | tf_op jit(solution)/shard_map/all_to_all | solution.py:15
  102.3 0.7 pad_maximum_fusion.1
  103.0 0.4 fusion.3
  103.4 11.1 %all-to-all-done.3 = f32[64,8,128]{2,1,0:T(8,128)} async-done(((f32[64,8,128]{2,1,0:T(8,128)}), f32[64,8,128]{2,1,0:T(8,128)}, u32[]{:S(2)}, u32[]{:S(2)}) %all-to-all-start.3) | async-done | bytes 262176 | tf_op jit(solution)/shard_map/all_to_all | solution.py:15
  114.5 1.0 reduce_sum.37
  115.6 0.1 copy.46
  115.7 0.1 pad_maximum_fusion.3
  115.8 6.1 %collective-permute-start.1 = (f32[16,32]{0,1:T(8,128)S(1)}, f32[16,32]{0,1:T(8,128)S(1)}, u32[]{:S(2)}, u32[]{:S(2)}) collective-permute-start(f32[16,32]{0,1:T(8,128)S(1)} %pad_maximum_fusion.3), channel_id=1, source_target_pairs={{0,64},{64,0},{1,65},{65,1},{2,66},{66,2},{3,67},{67,3},{4,68},{68... | collective-permute-start | bytes 6152 | tf_op jit(solution)/shard_map/ppermute | solution.py:27
  121.9 0.5 convolution_add_fusion.2
  122.4 0.1 slice_add_fusion
  122.5 1.9 collective-permute-start.2
  124.5 0.1 broadcast_select_fusion.3
  124.5 0.1 pad_maximum_fusion.4
  124.7 0.1 fusion.48
  124.8 2.9 %cholesky.17 = f32[32,32]{1,0:T(8,128)S(1)} custom-call(f32[32,32]{1,0:T(8,128)S(1)} %fusion.48), custom_call_target="Cholesky" | custom-call | tf_op jit(solution)/shard_map/jit(cholesky)/cholesky | solution.py:119
  127.8 0.2 reshape.133
  128.0 1.1 copy.48
  129.1 5.4 %all-to-all-start.4 = ((f32[64,16,96]{2,1,0:T(8,128)}), f32[64,16,96]{2,1,0:T(8,128)S(1)}, u32[]{:S(2)}, u32[]{:S(2)}) async-start(f32[64,16,96]{2,1,0:T(8,128)} %bitcast.64), calls=%async_computation.4 | async-start | bytes 1048576 | tf_op jit(solution)/shard_map/all_to_all | solution.py:15
  134.6 0.6 compare_reduce_fusion
  135.2 0.7 fusion.21
  135.9 2.4 %custom-call.6 = f32[1,32,32]{1,2,0:T(8,128)S(1)} custom-call(f32[1,32,32]{2,1,0:T(8,128)S(1)} %fusion.21), custom_call_target="InvertDiagBlocksLowerTriangular" | custom-call | tf_op jit(solution)/shard_map/triangular_solve | solution.py:120
  138.3 0.2 fusion.46
  138.5 0.1 fusion.51
  138.7 18.7 %all-to-all-done.4 = f32[64,16,96]{2,1,0:T(8,128)S(1)} async-done(((f32[64,16,96]{2,1,0:T(8,128)}), f32[64,16,96]{2,1,0:T(8,128)S(1)}, u32[]{:S(2)}, u32[]{:S(2)}) %all-to-all-start.4) | async-done | bytes 393248 | tf_op jit(solution)/shard_map/all_to_all | solution.py:15
  157.3 0.1 reduce_sum.38
  157.4 0.6 broadcast_in_dim.63
  158.0 5.5 %all-to-all-start.5 = ((f32[8,16,96]{2,1,0:T(8,128)}), f32[8,16,96]{2,1,0:T(8,128)S(1)}, u32[]{:S(2)}, u32[]{:S(2)}) async-start(f32[8,16,96]{2,1,0:T(8,128)} %broadcast_in_dim.63), calls=%async_computation.5 | async-start | bytes 131072 | tf_op jit(solution)/shard_map/all_to_all | solution.py:15
  163.5 7.5 %all-to-all-done.5 = f32[8,16,96]{2,1,0:T(8,128)S(1)} async-done(((f32[8,16,96]{2,1,0:T(8,128)}), f32[8,16,96]{2,1,0:T(8,128)S(1)}, u32[]{:S(2)}, u32[]{:S(2)}) %all-to-all-start.5) | async-done | bytes 49184 | tf_op jit(solution)/shard_map/all_to_all | solution.py:15
  171.0 0.8 reduce-precision_convert_fusion
  171.8 0.9 broadcast_in_dim.64
  172.6 5.5 %all-to-all-start.6 = ((bf16[64,32,96]{2,1,0:T(8,128)(2,1)}), bf16[64,32,96]{2,1,0:T(8,128)(2,1)S(1)}, u32[]{:S(2)}, u32[]{:S(2)}) async-start(bf16[64,32,96]{2,1,0:T(8,128)(2,1)} %broadcast_in_dim.64), calls=%async_computation.6 | async-start | bytes 1048576 | tf_op jit(solution)/shard_map/all_to_all | solution.py:15
  178.1 8.1 %convolution_add_fusion.1 = f32[128,6144]{1,0:T(8,128)} fusion(bf16[1024,128]{1,0:T(8,128)(2,1)S(1)} %bitcast.71, bf16[1024,6144]{1,0:T(8,128)(2,1)} %all-gather.2.cloned.1.call-done, bf16[1,128,6144]{2,1,0:T(8,128)(2,1)S(1)} %copy-done), kind=kOutput, calls=%fused_computation.2 | convolution fusion | flops 1612185600 | bytes 17563648 | tf_op jit(solution)/shard_map/dot_general | solution.py:46
  186.2 7.5 %all-to-all-done.6 = bf16[64,32,96]{2,1,0:T(8,128)(2,1)S(1)} async-done(((bf16[64,32,96]{2,1,0:T(8,128)(2,1)}), bf16[64,32,96]{2,1,0:T(8,128)(2,1)S(1)}, u32[]{:S(2)}, u32[]{:S(2)}) %all-to-all-start.6) | async-done | bytes 393248 | tf_op jit(solution)/shard_map/all_to_all | solution.py:15
  193.8 0.2 copy.42
  194.0 0.7 reshape.135
  194.7 4.5 %collective-permute-start.3 = (bf16[32,6144]{1,0:T(8,128)(2,1)S(1)}, bf16[32,6144]{1,0:T(8,128)(2,1)S(1)}, u32[]{:S(2)}, u32[]{:S(2)}) collective-permute-start(bf16[32,6144]{1,0:T(8,128)(2,1)S(1)} %reshape.135), channel_id=1, source_target_pairs={{0,64},{64,0},{1,65},{65,1},{2,66},{66,2},{3,67},{67,3},{4,68},{68... | collective-permute-start | bytes 1179656 | tf_op jit(solution)/shard_map/ppermute | solution.py:27
  199.3 1.3 collective-permute-done.3
  200.6 0.6 fusion.38
  201.2 1.3 copy-done.1
  202.5 1.7 fusion.2
  (42 shorter events, 1.0 us)
Async XLA Ops:
  7.2 170.9 %all-gather.2.cloned.1.call-start = ((), (), s32[]{:S(2)}) async-start(), calls=%async_computation.7 | async-start | bytes 12976128 | tf_op jit(solution)/shard_map/all_gather | solution.py:71
  7.2 8.1 %collective-permute-start = (bf16[16,6144]{1,0:T(8,128)(2,1)}, bf16[16,6144]{1,0:T(8,128)(2,1)S(1)}, u32[]{:S(2)}, u32[]{:S(2)}) collective-permute-start(bf16[16,6144]{1,0:T(8,128)(2,1)} %bitcast.69), channel_id=1, source_target_pairs={{0,32},{32,0},{1,33},{33,1},{2,34},{34,2},{3,35},{35,3},{4,36},{36... | collective-permute-start | bytes 589832 | tf_op jit(solution)/shard_map/ppermute | solution.py:23
  18.6 28.4 %copy-start.2 = (bf16[1,16,6144]{2,1,0:T(8,128)(2,1)S(1)}, bf16[1,16,6144]{2,1,0:T(8,128)(2,1)}, u32[]{:S(2)}) copy-start(bf16[1,16,6144]{2,1,0:T(8,128)(2,1)} %param.7) | copy-start | bytes 589828
  18.6 27.5 %all-to-all-start = ((bf16[64,32,96]{2,1,0:T(8,128)(2,1)}), bf16[64,32,96]{2,1,0:T(8,128)(2,1)S(1)}, u32[]{:S(2)}, u32[]{:S(2)}) async-start(bf16[64,32,96]{2,1,0:T(8,128)(2,1)} %broadcast_in_dim.27), calls=%async_computation | async-start | bytes 1048576 | tf_op jit(solution)/shard_map/all_to_all | solution.py:15
  46.1 11.1 %copy-start.5 = (f32[1,1024]{1,0:T(1,128)S(1)}, f32[1,1024]{1,0:T(1,128)}, u32[]{:S(2)}) copy-start(f32[1,1024]{1,0:T(1,128)} %param.8) | copy-start | bytes 12292
  46.1 22.0 %copy-start.4 = (bf16[1,1024,128]{2,1,0:T(8,128)(2,1)S(1)}, bf16[1,1024,128]{2,1,0:T(8,128)(2,1)}, u32[]{:S(2)}) copy-start(bf16[1,1024,128]{2,1,0:T(8,128)(2,1)} %param.6) | copy-start | bytes 786436
  46.3 22.2 %copy-start = (bf16[1,128,6144]{2,1,0:T(8,128)(2,1)S(1)}, bf16[1,128,6144]{2,1,0:T(8,128)(2,1)}, u32[]{:S(2)}) copy-start(bf16[1,128,6144]{2,1,0:T(8,128)(2,1)} %param.10) | copy-start | bytes 4718596
  48.1 20.0 %all-to-all-start.1 = ((bf16[64,16,128]{2,1,0:T(8,128)(2,1)}), bf16[64,16,128]{2,1,0:T(8,128)(2,1)S(1)}, u32[]{:S(2)}, u32[]{:S(2)}) async-start(bf16[64,16,128]{2,1,0:T(8,128)(2,1)} %broadcast_in_dim.29), calls=%async_computation.1 | async-start | bytes 524288 | tf_op jit(solution)/shard_map/all_to_all | solution.py:15
  69.9 24.5 %all-to-all-start.2 = ((f32[8,128,32]{1,2,0:T(8,128)}), f32[8,128,32]{1,2,0:T(8,128)S(1)}, u32[]{:S(2)}, u32[]{:S(2)}) async-start(f32[8,128,32]{1,2,0:T(8,128)} %broadcast_in_dim.30), calls=%async_computation.2 | async-start | bytes 262144 | tf_op jit(solution)/shard_map/all_to_all | solution.py:15
  96.2 18.3 %all-to-all-start.3 = ((f32[64,8,128]{2,1,0:T(8,128)}), f32[64,8,128]{2,1,0:T(8,128)}, u32[]{:S(2)}, u32[]{:S(2)}) async-start(f32[64,8,128]{2,1,0:T(8,128)} %pad_maximum_fusion.2), calls=%async_computation.3 | async-start | bytes 524288 | tf_op jit(solution)/shard_map/all_to_all | solution.py:15
  115.8 8.7 %collective-permute-start.1 = (f32[16,32]{0,1:T(8,128)S(1)}, f32[16,32]{0,1:T(8,128)S(1)}, u32[]{:S(2)}, u32[]{:S(2)}) collective-permute-start(f32[16,32]{0,1:T(8,128)S(1)} %pad_maximum_fusion.3), channel_id=1, source_target_pairs={{0,64},{64,0},{1,65},{65,1},{2,66},{66,2},{3,67},{67,3},{4,68},{68... | collective-permute-start | bytes 6152 | tf_op jit(solution)/shard_map/ppermute | solution.py:27
  122.5 5.2 %collective-permute-start.2 = (f32[16,6144]{1,0:T(8,128)S(1)}, f32[16,6144]{1,0:T(8,128)S(1)}, u32[]{:S(2)}, u32[]{:S(2)}) collective-permute-start(f32[16,6144]{1,0:T(8,128)S(1)} %slice_select_fusion), channel_id=1, source_target_pairs={{0,64},{64,0},{1,65},{65,1},{2,66},{66,2},{3,67},{67,3},{4,68},{68... | collective-permute-start | bytes 1179656 | tf_op jit(solution)/shard_map/ppermute | solution.py:27
  129.1 28.2 %all-to-all-start.4 = ((f32[64,16,96]{2,1,0:T(8,128)}), f32[64,16,96]{2,1,0:T(8,128)S(1)}, u32[]{:S(2)}, u32[]{:S(2)}) async-start(f32[64,16,96]{2,1,0:T(8,128)} %bitcast.64), calls=%async_computation.4 | async-start | bytes 1048576 | tf_op jit(solution)/shard_map/all_to_all | solution.py:15
  134.6 43.6 %copy-start.3 = (bf16[32,2,16,128]{3,2,1,0:T(8,128)(2,1)S(1)}, bf16[32,2,16,128]{3,2,1,0:T(8,128)(2,1)}, u32[]{:S(2)}) copy-start(bf16[32,2,16,128]{3,2,1,0:T(8,128)(2,1)} %pad_maximum_fusion.1) | copy-start | bytes 786436
  158.0 12.9 %all-to-all-start.5 = ((f32[8,16,96]{2,1,0:T(8,128)}), f32[8,16,96]{2,1,0:T(8,128)S(1)}, u32[]{:S(2)}, u32[]{:S(2)}) async-start(f32[8,16,96]{2,1,0:T(8,128)} %broadcast_in_dim.63), calls=%async_computation.5 | async-start | bytes 131072 | tf_op jit(solution)/shard_map/all_to_all | solution.py:15
  172.6 21.1 %all-to-all-start.6 = ((bf16[64,32,96]{2,1,0:T(8,128)(2,1)}), bf16[64,32,96]{2,1,0:T(8,128)(2,1)S(1)}, u32[]{:S(2)}, u32[]{:S(2)}) async-start(bf16[64,32,96]{2,1,0:T(8,128)(2,1)} %broadcast_in_dim.64), calls=%async_computation.6 | async-start | bytes 1048576 | tf_op jit(solution)/shard_map/all_to_all | solution.py:15
  194.7 5.9 %collective-permute-start.3 = (bf16[32,6144]{1,0:T(8,128)(2,1)S(1)}, bf16[32,6144]{1,0:T(8,128)(2,1)S(1)}, u32[]{:S(2)}, u32[]{:S(2)}) collective-permute-start(bf16[32,6144]{1,0:T(8,128)(2,1)S(1)} %reshape.135), channel_id=1, source_target_pairs={{0,64},{64,0},{1,65},{65,1},{2,66},{66,2},{3,67},{67,3},{4,68},{68... | collective-permute-start | bytes 1179656 | tf_op jit(solution)/shard_map/ppermute | solution.py:27
  200.6 1.9 copy-start.1
Sparse Core Ops, SparseCore 0:
  17.2 149.2 all-gather.1

commit v7 on v5

--- a/solution.py
+++ b/solution.py
@@ -25,6 +25,15 @@
 
 def swap_core(values):
     return lax.ppermute(values, "core", [(0, 1), (1, 0)])
+
+
+def arrange(values, own_first):
+    slots, units = values.shape
+    plane = lax.axis_size(PLANE)
+    parts = values.reshape(2, plane, slots // (2 * plane), units)
+    return jnp.stack(
+        [jnp.where(own_first, parts[0], parts[1]), jnp.where(own_first, parts[1], parts[0])], axis=1
+    ).reshape(slots, units)
 
 
 def fold(blocks):
@@ -67,9 +76,16 @@
     slot_scale = jnp.where(live_slots, gate_weight[0], jnp.zeros_like(gate_weight[0]))
     weighted = (hidden_local.astype(f32) * slot_scale[:, None]).astype(bf16)
 
-    pair_rows = jnp.concatenate([grad_rows, swap(grad_rows)], axis=0)
+    own_first = lax.axis_index("zl") == 0
+    half = width // 2
+    left_cols, right_cols = grad_rows[:, :half], grad_rows[:, half:]
+    kept_rows = jnp.where(own_first, left_cols, right_cols)
+    pair_rows = jnp.concatenate(
+        [kept_rows, swap(jnp.where(own_first, right_cols, left_cols))], axis=0
+    )
     query_blocks, pair_rows = lax.optimization_barrier((query_blocks, pair_rows))
-    full_grad = lax.all_gather(pair_rows, PLANE, axis=0, tiled=True)
+    half_grad = lax.all_gather(pair_rows, PLANE, axis=0, tiled=True)
+    partner_weighted = swap(weighted)
     full_query = query_blocks.transpose(1, 0, 2).reshape(rank, width)
 
     slot_query = product(grad_rows, full_query, 1, 1)
@@ -115,6 +131,9 @@
     incoming = exchange(core_part, DP)
     own_part = jnp.sum(incoming, axis=0)
     expert_parts = spread(own_part, EXPERT, replicas)
+    sent_grad = product(arrange(partner_weighted, own_first), half_grad, 0, 0).astype(bf16)
+    expert_parts, sent_grad = lax.optimization_barrier((expert_parts, sent_grad))
+    partner_grad = swap(sent_grad).astype(f32)
     own_sum = jnp.sum(expert_parts.reshape(-1, rank, own_rows), axis=0) / replicas
 
     chol_lower = jnp.linalg.cholesky(gram_matrix)
@@ -134,12 +153,17 @@
     )
     col_blocks = spread(sent_cols, DP, members)
 
-    own_first = lax.axis_index("zl") == 0
-    parts = weighted.reshape(2, lax.axis_size(PLANE), own_slots, units)
-    ordered = jnp.stack(
-        [jnp.where(own_first, parts[0], parts[1]), jnp.where(own_first, parts[1], parts[0])], axis=1
-    ).reshape(slots, units)
-    merged = product(ordered, full_grad, 0, 0) + error_local.astype(f32)
+    kept_grad = product(arrange(weighted, own_first), half_grad, 0, 0)
+    merged = (
+        jnp.concatenate(
+            [
+                jnp.where(own_first, kept_grad, partner_grad),
+                jnp.where(own_first, partner_grad, kept_grad),
+            ],
+            axis=1,
+        )
+        + error_local.astype(f32)
+    )
     merged, col_blocks = lax.optimization_barrier((merged, col_blocks))
     core_cols = col_blocks.transpose(1, 0, 2).reshape(rank, width)
     all_cols = jnp.concatenate([core_cols, swap_core(core_cols)], axis=0)

time: 212 us -> 203 us (0.958)
  waiting for transfers between devices: 95 us -> 74.2 us
  starting transfers between devices: 65.9 us -> 74.6 us
    all_gather x1, waiting for transfers between devices: 25.3 us -> 0.01 us  [body(): half_grad = lax.all_gather(pair_rows, PLANE, axis=0, tiled=True)]
    ppermute x1 -> x3, waiting for transfers between devices: 0.01 us -> 19.5 us  [swap(): return lax.ppermute(values, 'zl', [(0, 1), (1, 0)])]
    all_to_all x7, waiting for transfers between devices: 68.4 us -> 53.4 us  [exchange(): return lax.all_to_all(blocks, axes, split_axis=0, concat_axis=0, tiled=True)]
    all_to_all x7, starting transfers between devices: 51.2 us -> 55 us  [exchange(): return lax.all_to_all(blocks, axes, split_axis=0, concat_axis=0, tiled=True)]
    ppermute x1 -> x3, starting transfers between devices: 4.96 us -> 7.95 us  [swap(): return lax.ppermute(values, 'zl', [(0, 1), (1, 0)])]
    dot_general x9 -> x10, matrix products: 12.8 us -> 14.2 us  [product(): lax.dot_general(left_side, right_side, (((left_dim,), (right_dim,)), ((),...]
  transfers between devices with their start and end apart: 12 -> 14, of which waited for: 8 -> 9; matrix products, arithmetic and copies ran while one was open for 14% -> 16% of each run, Pallas kernels for 0% -> 0%
where the time goes in v7:
time: 203 us; the launch traced here: 202 us
  starting transfers between devices  74.6 us (37%)
  waiting for transfers between devices  74.2 us (37%)
  matrix products  15.4 us (8%)
  between operations  15.1 us (7%)
  other arithmetic  13.9 us (7%)
  local copies, waits for them, and re-layouts  8.97 us (4%)
    all_to_all x7, starting transfers between devices, exchange(): return lax.all_to_all(blocks, axes, split_axis=0, concat_axis=0, tiled=True)  55 us
    all_to_all x7, waiting for transfers between devices, exchange(): return lax.all_to_all(blocks, axes, split_axis=0, concat_axis=0, tiled=True)  53.4 us
    ppermute x3, waiting for transfers between devices, swap(): return lax.ppermute(values, 'zl', [(0, 1), (1, 0)])  19.5 us
    dot_general x10, matrix products, product(): lax.dot_general(left_side, right_side, (((left_dim,), (right_dim,)), ((),...  14.2 us
    ppermute x3, starting transfers between devices, swap_core(): return lax.ppermute(values, 'core', [(0, 1), (1, 0)])  11.6 us
    ppermute x3, starting transfers between devices, swap(): return lax.ppermute(values, 'zl', [(0, 1), (1, 0)])  7.95 us
  transfers between devices with their start and end apart: 14, of which 9 were waited for; matrix products, arithmetic and copies ran while one was open for 16% of the time, Pallas kernels for 0%

profile of v7, /device:TPU:1, one launch (start us, length us, event | category | flops | bytes accessed | tf_op | source)
XLA Modules:
  0.0 202.1 jit_solution(13752671060844779614)
XLA Ops:
  7.2 0.8 convert_bitcast_fusion.1
  7.9 0.9 broadcast_in_dim.27
  8.8 12.9 %all-to-all-start = ((bf16[64,32,96]{2,1,0:T(8,128)(2,1)}), bf16[64,32,96]{2,1,0:T(8,128)(2,1)S(1)}, u32[]{:S(2)}, u32[]{:S(2)}) async-start(bf16[64,32,96]{2,1,0:T(8,128)(2,1)} %broadcast_in_dim.27), calls=%async_computation | async-start | bytes 1048576 | tf_op jit(solution)/shard_map/all_to_all | solution.py:15
  21.8 3.0 %collective-permute-start = (bf16[16,3072]{1,0:T(8,128)(2,1)S(1)}, bf16[16,3072]{1,0:T(8,128)(2,1)S(1)}, u32[]{:S(2)}, u32[]{:S(2)}) collective-permute-start(bf16[16,3072]{1,0:T(8,128)(2,1)S(1)} %get-tuple-element.23), channel_id=1, source_target_pairs={{0,32},{32,0},{1,33},{33,1},{2,34},{34,2},{3,35},{35,3},{4,36},{36... | collective-permute-start | bytes 294920 | tf_op jit(solution)/shard_map/ppermute | solution.py:23
  24.9 4.7 %collective-permute-done = bf16[16,3072]{1,0:T(8,128)(2,1)S(1)} collective-permute-done((bf16[16,3072]{1,0:T(8,128)(2,1)S(1)}, bf16[16,3072]{1,0:T(8,128)(2,1)S(1)}, u32[]{:S(2)}, u32[]{:S(2)}) %collective-permute-start) | collective-permute-done | bytes 98336 | tf_op jit(solution)/shard_map/ppermute | solution.py:23
  29.5 0.7 pad_maximum_fusion.3
  30.2 7.4 %all-to-all-done = bf16[64,32,96]{2,1,0:T(8,128)(2,1)S(1)} async-done(((bf16[64,32,96]{2,1,0:T(8,128)(2,1)}), bf16[64,32,96]{2,1,0:T(8,128)(2,1)S(1)}, u32[]{:S(2)}, u32[]{:S(2)}) %all-to-all-start) | async-done | bytes 393248 | tf_op jit(solution)/shard_map/all_to_all | solution.py:15
  37.8 0.2 copy.32
  38.0 0.7 reshape.176
  38.7 0.2 reduce-precision_convert_fusion.5
  39.0 0.1 maximum_maximum_fusion
  39.1 0.8 broadcast_in_dim.29
  39.8 6.9 %all-to-all-start.1 = ((bf16[64,16,128]{2,1,0:T(8,128)(2,1)}), bf16[64,16,128]{2,1,0:T(8,128)(2,1)S(1)}, u32[]{:S(2)}, u32[]{:S(2)}) async-start(bf16[64,16,128]{2,1,0:T(8,128)(2,1)} %broadcast_in_dim.29), calls=%async_computation.1 | async-start | bytes 524288 | tf_op jit(solution)/shard_map/all_to_all | solution.py:15
  47.4 0.2 fusion.14
  47.6 3.0 %collective-permute-start.2 = (bf16[1024,128]{1,0:T(8,128)(2,1)S(1)}, bf16[1024,128]{1,0:T(8,128)(2,1)S(1)}, u32[]{:S(2)}, u32[]{:S(2)}) collective-permute-start(bf16[1024,128]{1,0:T(8,128)(2,1)S(1)} %fusion.14), channel_id=1, source_target_pairs={{0,32},{32,0},{1,33},{33,1},{2,34},{34,2},{3,35},{35,3},{4,36},{36... | collective-permute-start | bytes 786440 | tf_op jit(solution)/shard_map/ppermute | solution.py:23
  50.6 6.8 %all-to-all-done.1 = bf16[64,16,128]{2,1,0:T(8,128)(2,1)S(1)} async-done(((bf16[64,16,128]{2,1,0:T(8,128)(2,1)}), bf16[64,16,128]{2,1,0:T(8,128)(2,1)S(1)}, u32[]{:S(2)}, u32[]{:S(2)}) %all-to-all-start.1) | async-done | bytes 262176 | tf_op jit(solution)/shard_map/all_to_all | solution.py:15
  57.4 0.4 fusion.21
  57.9 0.6 fusion.10
  58.5 0.7 broadcast_in_dim.30
  59.2 13.1 %all-to-all-start.2 = ((f32[8,128,32]{1,2,0:T(8,128)}), f32[8,128,32]{1,2,0:T(8,128)S(1)}, u32[]{:S(2)}, u32[]{:S(2)}) async-start(f32[8,128,32]{1,2,0:T(8,128)} %broadcast_in_dim.30), calls=%async_computation.2 | async-start | bytes 262144 | tf_op jit(solution)/shard_map/all_to_all | solution.py:15
  72.3 8.0 %all-to-all-done.2 = f32[8,128,32]{1,2,0:T(8,128)S(1)} async-done(((f32[8,128,32]{1,2,0:T(8,128)}), f32[8,128,32]{1,2,0:T(8,128)S(1)}, u32[]{:S(2)}, u32[]{:S(2)}) %all-to-all-start.2) | async-done | bytes 131104 | tf_op jit(solution)/shard_map/all_to_all | solution.py:15
  80.3 0.3 fusion.16
  80.6 0.1 fusion.56
  81.2 0.9 pad_maximum_fusion.1
  82.1 5.9 %all-to-all-start.3 = ((f32[64,8,128]{2,1,0:T(8,128)}), f32[64,8,128]{2,1,0:T(8,128)}, u32[]{:S(2)}, u32[]{:S(2)}) async-start(f32[64,8,128]{2,1,0:T(8,128)} %pad_maximum_fusion.1), calls=%async_computation.3 | async-start | bytes 524288 | tf_op jit(solution)/shard_map/all_to_all | solution.py:15
  88.0 0.7 pad_maximum_fusion.2
  88.8 0.4 fusion.3
  89.1 9.5 %all-to-all-done.3 = f32[64,8,128]{2,1,0:T(8,128)} async-done(((f32[64,8,128]{2,1,0:T(8,128)}), f32[64,8,128]{2,1,0:T(8,128)}, u32[]{:S(2)}, u32[]{:S(2)}) %all-to-all-start.3) | async-done | bytes 262176 | tf_op jit(solution)/shard_map/all_to_all | solution.py:15
  98.6 1.0 reduce_sum.37
  99.7 0.1 copy.46
  100.0 5.5 %collective-permute-start.4 = (f32[16,32]{0,1:T(8,128)S(1)}, f32[16,32]{0,1:T(8,128)S(1)}, u32[]{:S(2)}, u32[]{:S(2)}) collective-permute-start(f32[16,32]{0,1:T(8,128)S(1)} %pad_maximum_fusion.4), channel_id=1, source_target_pairs={{0,64},{64,0},{1,65},{65,1},{2,66},{66,2},{3,67},{67,3},{4,68},{68... | collective-permute-start | bytes 6152 | tf_op jit(solution)/shard_map/ppermute | solution.py:27
  105.5 1.4 convolution_add_fusion.1
  106.9 0.1 slice_add_fusion
  107.0 1.9 collective-permute-start.1
  109.2 0.1 fusion.51
  109.3 2.9 %cholesky.17 = f32[32,32]{1,0:T(8,128)S(1)} custom-call(f32[32,32]{1,0:T(8,128)S(1)} %fusion.51), custom_call_target="Cholesky" | custom-call | tf_op jit(solution)/shard_map/jit(cholesky)/cholesky | solution.py:139
  112.3 0.2 reshape.179
  112.5 1.1 copy.48
  113.6 4.6 %all-to-all-start.4 = ((f32[64,16,96]{2,1,0:T(8,128)}), f32[64,16,96]{2,1,0:T(8,128)S(1)}, u32[]{:S(2)}, u32[]{:S(2)}) async-start(f32[64,16,96]{2,1,0:T(8,128)} %bitcast.77), calls=%async_computation.4 | async-start | bytes 1048576 | tf_op jit(solution)/shard_map/all_to_all | solution.py:15
  118.2 0.6 compare_reduce_fusion
  118.9 0.7 fusion.24
  119.5 2.4 %custom-call.6 = f32[1,32,32]{1,2,0:T(8,128)S(1)} custom-call(f32[1,32,32]{2,1,0:T(8,128)S(1)} %fusion.24), custom_call_target="InvertDiagBlocksLowerTriangular" | custom-call | tf_op jit(solution)/shard_map/triangular_solve | solution.py:140
  122.0 0.2 fusion.49
  122.2 0.1 fusion.54
  122.3 18.9 %all-to-all-done.4 = f32[64,16,96]{2,1,0:T(8,128)S(1)} async-done(((f32[64,16,96]{2,1,0:T(8,128)}), f32[64,16,96]{2,1,0:T(8,128)S(1)}, u32[]{:S(2)}, u32[]{:S(2)}) %all-to-all-start.4) | async-done | bytes 393248 | tf_op jit(solution)/shard_map/all_to_all | solution.py:15
  141.3 0.1 reduce_sum.38
  141.3 0.6 broadcast_in_dim.63
  142.0 5.1 %all-to-all-start.5 = ((f32[8,16,96]{2,1,0:T(8,128)}), f32[8,16,96]{2,1,0:T(8,128)S(1)}, u32[]{:S(2)}, u32[]{:S(2)}) async-start(f32[8,16,96]{2,1,0:T(8,128)} %broadcast_in_dim.63), calls=%async_computation.5 | async-start | bytes 131072 | tf_op jit(solution)/shard_map/all_to_all | solution.py:15
  147.1 4.7 %convolution_convert_fusion = bf16[128,3072]{1,0:T(8,128)(2,1)} fusion(bf16[1024,128]{1,0:T(8,128)(2,1)S(1)} %bitcast.83, bf16[1024,3072]{1,0:T(8,128)(2,1)} %all-gather.2.cloned.1.call-done), kind=kOutput, calls=%fused_computation.5 | convolution fusion | flops 805699584 | bytes 7340032 | tf_op jit(solution)/shard_map/dot_general | solution.py:55
  151.8 2.8 %all-to-all-done.5 = f32[8,16,96]{2,1,0:T(8,128)S(1)} async-done(((f32[8,16,96]{2,1,0:T(8,128)}), f32[8,16,96]{2,1,0:T(8,128)S(1)}, u32[]{:S(2)}, u32[]{:S(2)}) %all-to-all-start.5) | async-done | bytes 49184 | tf_op jit(solution)/shard_map/all_to_all | solution.py:15
  154.6 1.9 collective-permute-start.3
  156.5 0.8 reduce-precision_convert_fusion
  157.3 0.9 broadcast_in_dim.64
  158.2 6.4 %all-to-all-start.6 = ((bf16[64,32,96]{2,1,0:T(8,128)(2,1)}), bf16[64,32,96]{2,1,0:T(8,128)(2,1)S(1)}, u32[]{:S(2)}, u32[]{:S(2)}) async-start(bf16[64,32,96]{2,1,0:T(8,128)(2,1)} %broadcast_in_dim.64), calls=%async_computation.6 | async-start | bytes 1048576 | tf_op jit(solution)/shard_map/all_to_all | solution.py:15
  164.6 14.8 %collective-permute-done.3 = bf16[128,3072]{1,0:T(8,128)(2,1)S(1)} collective-permute-done((bf16[128,3072]{1,0:T(8,128)(2,1)}, bf16[128,3072]{1,0:T(8,128)(2,1)S(1)}, u32[]{:S(2)}, u32[]{:S(2)}) %collective-permute-start.3) | collective-permute-done | bytes 786464 | tf_op jit(solution)/shard_map/ppermute | solution.py:23
  179.4 3.8 %convert_select_fusion.1 = (f32[128,3072]{1,0:T(8,128)S(1)}, f32[128,3072]{1,0:T(8,128)S(1)}) fusion(bf16[128,3072]{1,0:T(8,128)(2,1)S(1)} %collective-permute-done.3, pred[]{:T(512)S(6)} %eq.7, bf16[1024,128]{1,0:T(8,128)(2,1)S(1)} %bitcast.82, bf16[1024,3072]{1,0:T(8,128)(2,1)} %all-gather.2.cloned.1.call-done), kind=kOutput, calls=%fused_computation.8 | convolution fusion | flops 806486016 | bytes 10485761 | tf_op jit(solution)/shard_map/dot_general | solution.py:55
  183.2 1.9 maximum_add_fusion
  185.1 0.2 copy.42
  185.3 0.7 reshape.182
  186.1 4.2 %collective-permute-start.5 = (bf16[32,6144]{1,0:T(8,128)(2,1)S(1)}, bf16[32,6144]{1,0:T(8,128)(2,1)S(1)}, u32[]{:S(2)}, u32[]{:S(2)}) collective-permute-start(bf16[32,6144]{1,0:T(8,128)(2,1)S(1)} %reshape.182), channel_id=1, source_target_pairs={{0,64},{64,0},{1,65},{65,1},{2,66},{66,2},{3,67},{67,3},{4,68},{68... | collective-permute-start | bytes 1179656 | tf_op jit(solution)/shard_map/ppermute | solution.py:27
  190.3 1.3 collective-permute-done.5
  191.6 0.6 fusion.41
  192.2 1.3 copy-done.1
  193.5 1.8 fusion.2
  (51 shorter events, 1.4 us)
Async XLA Ops:
  7.2 14.6 %copy-start.3 = (bf16[1,16,6144]{2,1,0:T(8,128)(2,1)S(1)}, bf16[1,16,6144]{2,1,0:T(8,128)(2,1)}, u32[]{:S(2)}) copy-start(bf16[1,16,6144]{2,1,0:T(8,128)(2,1)} %param.7) | copy-start | bytes 589828
  8.8 28.9 %all-to-all-start = ((bf16[64,32,96]{2,1,0:T(8,128)(2,1)}), bf16[64,32,96]{2,1,0:T(8,128)(2,1)S(1)}, u32[]{:S(2)}, u32[]{:S(2)}) async-start(bf16[64,32,96]{2,1,0:T(8,128)(2,1)} %broadcast_in_dim.27), calls=%async_computation | async-start | bytes 1048576 | tf_op jit(solution)/shard_map/all_to_all | solution.py:15
  21.7 125.4 %all-gather.2.cloned.1.call-start = ((), (), s32[]{:S(2)}) async-start(), calls=%async_computation.7 | async-start | bytes 6488064 | tf_op jit(solution)/shard_map/all_gather | solution.py:87
  21.8 7.7 %collective-permute-start = (bf16[16,3072]{1,0:T(8,128)(2,1)S(1)}, bf16[16,3072]{1,0:T(8,128)(2,1)S(1)}, u32[]{:S(2)}, u32[]{:S(2)}) collective-permute-start(bf16[16,3072]{1,0:T(8,128)(2,1)S(1)} %get-tuple-element.23), channel_id=1, source_target_pairs={{0,32},{32,0},{1,33},{33,1},{2,34},{34,2},{3,35},{35,3},{4,36},{36... | collective-permute-start | bytes 294920 | tf_op jit(solution)/shard_map/ppermute | solution.py:23
  37.8 9.6 %copy-start.5 = (f32[1,1024]{1,0:T(1,128)S(1)}, f32[1,1024]{1,0:T(1,128)}, u32[]{:S(2)}) copy-start(f32[1,1024]{1,0:T(1,128)} %param.8) | copy-start | bytes 12292
  37.8 9.6 %copy-start.4 = (bf16[1,1024,128]{2,1,0:T(8,128)(2,1)S(1)}, bf16[1,1024,128]{2,1,0:T(8,128)(2,1)}, u32[]{:S(2)}) copy-start(bf16[1,1024,128]{2,1,0:T(8,128)(2,1)} %param.6) | copy-start | bytes 786436
  38.0 19.9 %copy-start = (bf16[1,128,6144]{2,1,0:T(8,128)(2,1)S(1)}, bf16[1,128,6144]{2,1,0:T(8,128)(2,1)}, u32[]{:S(2)}) copy-start(bf16[1,128,6144]{2,1,0:T(8,128)(2,1)} %param.10) | copy-start | bytes 4718596
  39.8 17.6 %all-to-all-start.1 = ((bf16[64,16,128]{2,1,0:T(8,128)(2,1)}), bf16[64,16,128]{2,1,0:T(8,128)(2,1)S(1)}, u32[]{:S(2)}, u32[]{:S(2)}) async-start(bf16[64,16,128]{2,1,0:T(8,128)(2,1)} %broadcast_in_dim.29), calls=%async_computation.1 | async-start | bytes 524288 | tf_op jit(solution)/shard_map/all_to_all | solution.py:15
  47.6 40.4 %collective-permute-start.2 = (bf16[1024,128]{1,0:T(8,128)(2,1)S(1)}, bf16[1024,128]{1,0:T(8,128)(2,1)S(1)}, u32[]{:S(2)}, u32[]{:S(2)}) collective-permute-start(bf16[1024,128]{1,0:T(8,128)(2,1)S(1)} %fusion.14), channel_id=1, source_target_pairs={{0,32},{32,0},{1,33},{33,1},{2,34},{34,2},{3,35},{35,3},{4,36},{36... | collective-permute-start | bytes 786440 | tf_op jit(solution)/shard_map/ppermute | solution.py:23
  59.2 21.1 %all-to-all-start.2 = ((f32[8,128,32]{1,2,0:T(8,128)}), f32[8,128,32]{1,2,0:T(8,128)S(1)}, u32[]{:S(2)}, u32[]{:S(2)}) async-start(f32[8,128,32]{1,2,0:T(8,128)} %broadcast_in_dim.30), calls=%async_computation.2 | async-start | bytes 262144 | tf_op jit(solution)/shard_map/all_to_all | solution.py:15
  82.1 16.5 %all-to-all-start.3 = ((f32[64,8,128]{2,1,0:T(8,128)}), f32[64,8,128]{2,1,0:T(8,128)}, u32[]{:S(2)}, u32[]{:S(2)}) async-start(f32[64,8,128]{2,1,0:T(8,128)} %pad_maximum_fusion.1), calls=%async_computation.3 | async-start | bytes 524288 | tf_op jit(solution)/shard_map/all_to_all | solution.py:15
  100.0 9.0 %collective-permute-start.4 = (f32[16,32]{0,1:T(8,128)S(1)}, f32[16,32]{0,1:T(8,128)S(1)}, u32[]{:S(2)}, u32[]{:S(2)}) collective-permute-start(f32[16,32]{0,1:T(8,128)S(1)} %pad_maximum_fusion.4), channel_id=1, source_target_pairs={{0,64},{64,0},{1,65},{65,1},{2,66},{66,2},{3,67},{67,3},{4,68},{68... | collective-permute-start | bytes 6152 | tf_op jit(solution)/shard_map/ppermute | solution.py:27
  107.0 5.2 %collective-permute-start.1 = (f32[16,6144]{1,0:T(8,128)S(1)}, f32[16,6144]{1,0:T(8,128)S(1)}, u32[]{:S(2)}, u32[]{:S(2)}) collective-permute-start(f32[16,6144]{1,0:T(8,128)S(1)} %slice_select_fusion), channel_id=1, source_target_pairs={{0,64},{64,0},{1,65},{65,1},{2,66},{66,2},{3,67},{67,3},{4,68},{68... | collective-permute-start | bytes 1179656 | tf_op jit(solution)/shard_map/ppermute | solution.py:27
  112.5 34.6 %copy-start.2 = (bf16[32,2,16,128]{3,2,1,0:T(8,128)(2,1)S(1)}, bf16[32,2,16,128]{3,2,1,0:T(8,128)(2,1)}, u32[]{:S(2)}) copy-start(bf16[32,2,16,128]{3,2,1,0:T(8,128)(2,1)} %pad_maximum_fusion.2) | copy-start | bytes 786436
  113.6 27.6 %all-to-all-start.4 = ((f32[64,16,96]{2,1,0:T(8,128)}), f32[64,16,96]{2,1,0:T(8,128)S(1)}, u32[]{:S(2)}, u32[]{:S(2)}) async-start(f32[64,16,96]{2,1,0:T(8,128)} %bitcast.77), calls=%async_computation.4 | async-start | bytes 1048576 | tf_op jit(solution)/shard_map/all_to_all | solution.py:15
  142.0 12.6 %all-to-all-start.5 = ((f32[8,16,96]{2,1,0:T(8,128)}), f32[8,16,96]{2,1,0:T(8,128)S(1)}, u32[]{:S(2)}, u32[]{:S(2)}) async-start(f32[8,16,96]{2,1,0:T(8,128)} %broadcast_in_dim.63), calls=%async_computation.5 | async-start | bytes 131072 | tf_op jit(solution)/shard_map/all_to_all | solution.py:15
  154.6 24.8 %collective-permute-start.3 = (bf16[128,3072]{1,0:T(8,128)(2,1)}, bf16[128,3072]{1,0:T(8,128)(2,1)S(1)}, u32[]{:S(2)}, u32[]{:S(2)}) collective-permute-start(bf16[128,3072]{1,0:T(8,128)(2,1)} %convolution_convert_fusion), channel_id=1, source_target_pairs={{0,32},{32,0},{1,33},{33,1},{2,34},{34,2},{3,35},{35,3},{4,36},{36... | collective-permute-start | bytes 2359304 | tf_op jit(solution)/shard_map/ppermute | solution.py:23
  158.2 27.0 %all-to-all-start.6 = ((bf16[64,32,96]{2,1,0:T(8,128)(2,1)}), bf16[64,32,96]{2,1,0:T(8,128)(2,1)S(1)}, u32[]{:S(2)}, u32[]{:S(2)}) async-start(bf16[64,32,96]{2,1,0:T(8,128)(2,1)} %broadcast_in_dim.64), calls=%async_computation.6 | async-start | bytes 1048576 | tf_op jit(solution)/shard_map/all_to_all | solution.py:15
  186.1 5.5 %collective-permute-start.5 = (bf16[32,6144]{1,0:T(8,128)(2,1)S(1)}, bf16[32,6144]{1,0:T(8,128)(2,1)S(1)}, u32[]{:S(2)}, u32[]{:S(2)}) collective-permute-start(bf16[32,6144]{1,0:T(8,128)(2,1)S(1)} %reshape.182), channel_id=1, source_target_pairs={{0,64},{64,0},{1,65},{65,1},{2,66},{66,2},{3,67},{67,3},{4,68},{68... | collective-permute-start | bytes 1179656 | tf_op jit(solution)/shard_map/ppermute | solution.py:27
  191.6 1.9 copy-start.1
Sparse Core Ops, SparseCore 0:
  37.8 105.6 all-gather.1
